TPU v7x, 512 devices: a whole 4x8x8 slice. The times are simulated.
512 devices in a mesh: dp: 128 (over y, z, core), seq: 4 (over x).
Axes of the slice: x: 4, y: 8, z: 8, core: 2. Of those that a mesh axis runs over, the one named last changes fastest.
Arguments:
- queries: bfloat16 [128, 512, 2048], P('dp', None, 'seq'), may hold values from -20 to 20
- key_states: bfloat16 [128, 512, 2048], P('dp', None, 'seq'), may hold values from -20 to 20
- value_states: bfloat16 [128, 512, 2048], P('dp', None, 'seq'), may hold values from -6 to 6
- grad_out: bfloat16 [128, 512, 4096], P('dp', 'seq'), may hold values from -6 to 6
- out_weight: bfloat16 [4096, 2048], P('dp', 'seq'), may hold values from -0.125 to 0.125
- depths: int32 [128, 512], P('dp'), may hold values from 1 to 4, as said below
- documents: int32 [128, 512], P('dp'), may hold values from 0 to 3, never falling along the last dimension, each value on 1 to 256 neighbouring positions
Outputs:
- grad_queries: bfloat16 [128, 512, 2048], P('dp', None, 'seq')
- grad_keys: bfloat16 [128, 512, 2048], P('dp', None, 'seq')
- grad_values: bfloat16 [128, 512, 2048], P('dp', None, 'seq')
Inputs may be any that keep to these rules, and one draw needn't show every extreme that they name: `depths`: in every block of 128 positions of a sequence (the positions of one index of seq) at most 64 tokens have depth 4; in every sequence some block has exactly 64.
All inputs are finite; a program needn't handle non-finite values.
Results may differ from a plain program's by a relative error of at most 0.017.
Values may be sent and summed in bfloat16 or wider, within the bound.
No kernel may reach another device: no remote copies, remote signals or barrier semaphores. Data moves between devices by JAX's collectives and lax.ppermute only.
A program may use at most 64 MiB of HBM per device.

v0:
```python
import jax
import jax.numpy as jnp
from jax import lax
from jax.sharding import PartitionSpec as P

HD = 128
RECUR = 4


def head_grads(queries, key_states, value_states, out_grad, allowed, alive_rows):
    row_count = queries.shape[0]
    head_count = queries.shape[1] // HD
    score_scale = HD ** (-0.5)
    query_h = queries.reshape(row_count, head_count, HD)
    key_h = key_states.reshape(row_count, head_count, HD)
    value_h = value_states.reshape(row_count, head_count, HD)
    grad_h = out_grad.reshape(row_count, head_count, HD)
    scores = (
        jnp.einsum("qhd,khd->hqk", query_h, key_h, preferred_element_type=jnp.float32) * score_scale
    )
    masked = jnp.where(allowed[None], scores, -1e30)
    row_max = jnp.where(alive_rows[None, :, None], jnp.max(masked, axis=2, keepdims=True), 0.0)
    weights_raw = jnp.where(allowed[None], jnp.exp(masked - row_max), 0.0)
    row_total = jnp.sum(weights_raw, axis=2, keepdims=True)
    row_total = jnp.where(alive_rows[None, :, None], row_total, 1.0)
    probabilities = weights_raw / row_total
    probs_b = probabilities.astype(jnp.bfloat16)
    attended = jnp.einsum("hqk,khd->qhd", probs_b, value_h, preferred_element_type=jnp.float32)
    row_delta = jnp.sum(grad_h.astype(jnp.float32) * attended, axis=2)
    grad_values = jnp.einsum("hqk,qhd->khd", probs_b, grad_h, preferred_element_type=jnp.float32)
    dprob = jnp.einsum("qhd,khd->hqk", grad_h, value_h, preferred_element_type=jnp.float32)
    dscore = (probabilities * (dprob - row_delta.T[:, :, None])).astype(jnp.bfloat16)
    grad_queries = (
        jnp.einsum("hqk,khd->qhd", dscore, key_h, preferred_element_type=jnp.float32) * score_scale
    )
    grad_keys = (
        jnp.einsum("hqk,qhd->khd", dscore, query_h, preferred_element_type=jnp.float32)
        * score_scale
    )
    width = head_count * HD
    return (
        grad_queries.reshape(row_count, width).astype(jnp.bfloat16),
        grad_keys.reshape(row_count, width).astype(jnp.bfloat16),
        grad_values.reshape(row_count, width).astype(jnp.bfloat16),
    )


def project_rows(cotangent_rows, out_weight):
    summed = jnp.dot(
        cotangent_rows,
        lax.all_gather(out_weight, "dp", axis=0, tiled=True),
        preferred_element_type=jnp.float32,
    )
    return summed.astype(jnp.bfloat16)


def on_device(queries, key_states, value_states, grad_out, out_weight, depths, documents):
    seq_len = queries.shape[1]
    alive_rows = depths[0] >= RECUR
    positions = jnp.arange(seq_len, dtype=jnp.int32)
    doc_ids = documents[0]
    cotangent_rows = lax.all_gather(grad_out[0], "seq", axis=0, tiled=True)
    out_grad = project_rows(cotangent_rows, out_weight)
    allowed = (
        alive_rows[:, None]
        & alive_rows[None, :]
        & (doc_ids[:, None] == doc_ids[None, :])
        & (positions[None, :] <= positions[:, None])
    )
    grad_queries, grad_keys, grad_values = head_grads(
        queries[0], key_states[0], value_states[0], out_grad, allowed, alive_rows
    )
    return (grad_queries[None], grad_keys[None], grad_values[None])


def solution(mesh):
    return jax.shard_map(
        on_device,
        mesh=mesh,
        in_specs=(
            P("dp", None, "seq"),
            P("dp", None, "seq"),
            P("dp", None, "seq"),
            P("dp", "seq", None),
            P("dp", "seq"),
            P("dp", None),
            P("dp", None),
        ),
        out_specs=(P("dp", None, "seq"), P("dp", None, "seq"), P("dp", None, "seq")),
        check_vma=False,
    )
```

profile of v0, /device:TPU:1, one launch (start us, length us, event | category | flops | bytes accessed | tf_op | source)
XLA Modules:
  0.0 180.0 jit_solution(9693857219293140580)
XLA Ops:
  7.2 0.0 copy-start.3
  7.2 0.0 copy-start.2
  7.2 0.0 all-gather.6.cloned.1.call-start
  7.2 0.7 all-gather.6.cloned.1.call-update
  7.9 0.0 all-gather.4.cloned.1.call-start
  8.0 0.7 all-gather.4.cloned.1.call-update
  8.7 1.3 copy.32
  9.9 1.3 copy.31
  11.2 1.3 copy.33
  12.4 0.0 copy-done.3
  12.5 0.0 copy-done.2
  12.5 0.3 fusion.14
  12.8 1.0 fusion.2
  13.7 0.0 copy-start
  13.7 2.0 %copy-done = f32[4,512,512]{1,2,0:T(8,128)} copy-done((f32[4,512,512]{1,2,0:T(8,128)}, f32[4,512,512]{1,2,0:T(8,128)S(1)}, u32[]{:S(2)}) %copy-start) | copy-done | bytes 4194328
  15.7 1.0 fusion.4
  16.8 52.5 %all-gather.6.cloned.1.call-done = bf16[1,512,4096]{2,1,0:T(8,128)(2,1)} async-done(((bf16[1,128,4096]{2,1,0:T(8,128)(2,1)}), bf16[1,512,4096]{2,1,0:T(8,128)(2,1)}) %all-gather.6.cloned.1.call-update) | async-done | bytes 4194320 | tf_op jit(solution)/shard_map/all_gather | solution.py:62
  69.2 88.6 %all-gather.4.cloned.1.call-done = bf16[4096,512]{1,0:T(8,128)(2,1)} async-done(((bf16[32,512]{1,0:T(8,128)(2,1)}), bf16[4096,512]{1,0:T(8,128)(2,1)}) %all-gather.4.cloned.1.call-update) | async-done | bytes 4194320 | tf_op jit(solution)/shard_map/all_gather | solution.py:51
  157.9 0.0 copy-start.1
  157.9 6.0 %fusion.6 = bf16[512,512]{0,1:T(8,128)(2,1)S(1)} fusion(bf16[4096,512]{1,0:T(8,128)(2,1)} %all-gather.4.cloned.1.call-done, bf16[1,512,4096]{2,1,0:T(8,128)(2,1)} %all-gather.6.cloned.1.call-done), kind=kOutput, calls=%fused_computation.12 | convolution fusion | flops 2147745792 | bytes 8912896 | tf_op jit(solution)/shard_map/dot_general | solution.py:49
  163.8 0.0 copy-done.1
  163.9 1.6 convolution_convert_fusion
  165.4 1.6 fusion.11
  167.1 1.8 multiply_convert_fusion
  168.9 0.8 fusion.9
  169.7 0.5 fusion.10
  170.2 1.0 copy.22
  171.2 1.0 copy.23
  172.2 1.0 copy.24
  (3 shorter events, 0.0 us)
Async XLA Ops:
  7.2 5.3 %copy-start.3 = (s32[1,512]{1,0:T(1,128)S(1)}, s32[1,512]{1,0:T(1,128)}, u32[]{:S(2)}) copy-start(s32[1,512]{1,0:T(1,128)} %param.12) | copy-start | bytes 6148
  7.2 5.3 %copy-start.2 = (s32[1,512]{1,0:T(1,128)S(1)}, s32[1,512]{1,0:T(1,128)}, u32[]{:S(2)}) copy-start(s32[1,512]{1,0:T(1,128)} %param.13) | copy-start | bytes 6148
  7.2 62.0 %all-gather.6.cloned.1.call-start = ((), (), s32[]{:S(2)}) async-start(), calls=%async_computation.1 | async-start | bytes 5242880 | tf_op jit(solution)/shard_map/all_gather | solution.py:62
  7.9 149.9 %all-gather.4.cloned.1.call-start = ((), (), s32[]{:S(2)}) async-start(), calls=%async_computation | async-start | bytes 4227072 | tf_op jit(solution)/shard_map/all_gather | solution.py:51
  13.7 2.0 %copy-start = (f32[4,512,512]{1,2,0:T(8,128)}, f32[4,512,512]{1,2,0:T(8,128)S(1)}, u32[]{:S(2)}) copy-start(f32[4,512,512]{1,2,0:T(8,128)S(1)} %get-tuple-element.7) | copy-start | bytes 12582916
  157.9 6.0 %copy-start.1 = (f32[4,512,512]{1,2,0:T(8,128)S(1)}, f32[4,512,512]{1,2,0:T(8,128)}, u32[]{:S(2)}) copy-start(f32[4,512,512]{1,2,0:T(8,128)} %copy-done) | copy-start | bytes 12582916
Sparse Core Ops, SparseCore 0:
  10.1 59.0 all-gather.5
  72.4 85.4 all-gather.3
where the time goes:
time: 180 us
  waiting for transfers between devices  142 us (79%)
  between operations  14.2 us (8%)
  matrix products  13.2 us (7%)
  local copies, waits for them, and re-layouts  8.75 us (5%)
    all_gather x1, waiting for transfers between devices, project_rows(): lax.all_gather(out_weight, 'dp', axis=0, tiled=True)  88.6 us
    all_gather x1, waiting for transfers between devices, on_device(): cotangent_rows = lax.all_gather(grad_out[0], 'seq', axis=0, tiled=True)  52.5 us
    dot_general x1, matrix products, project_rows(): jnp.dot(cotangent_rows, lax.all_gather(out_weight, 'dp', axis=0, tiled=Tr...  5.97 us
    unnamed x11, local copies, waits for them, and re-layouts  4.98 us
  transfers between devices with their start and end apart: 2, of which 2 were waited for; matrix products, arithmetic and copies ran while one was open for 3% of the time, Pallas kernels for 0%

commit v1 on v0

v1 whole, which is shorter than its diff:
```python
import functools

import jax
import jax.numpy as jnp
from jax import lax
from jax.experimental import pallas as pl
from jax.experimental.pallas import tpu as pltpu
from jax.sharding import PartitionSpec as P

HD = 128
RECUR = 4
GROUP = 128
CAP = 64
NX, NY, NZ = 4, 8, 8
SEQ = NX * GROUP
ROWS = NX * CAP
D = NY * NZ * 64
YB = D // NY
HALF = YB // 2
KC = D // 2
COLS = 512
HEADS = COLS // HD
VMEM = 48 * 1024 * 1024
NT = (((1,), (1,)), ((), ()))
TN = (((0,), (0,)), ((), ()))
bf16, f32 = jnp.bfloat16, jnp.float32


def _place(y, z, c):
    return ((y % NY) * NZ + z % NZ) * 2 + c


_ALL = [(y, z, c) for y in range(NY) for z in range(NZ) for c in range(2)]
Z_GROUPS = [[_place(y, z, c) for z in range(NZ)] for y in range(NY) for c in range(2)]
SWAP = [(_place(y, z, c), _place(y, z, 1 - c)) for y, z, c in _ALL]
ALONG = [(_place(y, z, c), _place(y + 1 - 2 * c, z, c)) for y, z, c in _ALL]
CROSS = [(_place(y, z, c), _place(y + 2 * c - 1, z, 1 - c)) for y, z, c in _ALL]
UP = [(i, (i + 1) % NX) for i in range(NX)]
DOWN = [(i, (i + NX - 1) % NX) for i in range(NX)]


def _dot(a, b, dims=(((1,), (0,)), ((), ()))):
    return lax.dot_general(a, b, dims, preferred_element_type=f32)


def _selection(depth_row):
    live = (depth_row >= RECUR).astype(f32)
    live8 = jnp.broadcast_to(live, (8, GROUP)).astype(bf16)
    before = (
        lax.broadcasted_iota(jnp.int32, (GROUP, GROUP), 0)
        < lax.broadcasted_iota(jnp.int32, (GROUP, GROUP), 1)
    ).astype(bf16)
    rank = _dot(live8, before)[0:1].astype(jnp.int32)
    rank = jnp.where(live > 0.0, rank, -1)
    slot = lax.broadcasted_iota(jnp.int32, (CAP, GROUP), 0)
    return (slot == rank).astype(bf16)


def _cotangent_kernel(depths_ref, grad_ref, keep_ref, send_ref):
    dp = lax.axis_index("dp")
    x = lax.axis_index("seq")
    core = lax.rem(dp, 2)
    y = lax.div(dp, 2 * NZ)
    step = 1 - 2 * core
    sel = _selection(depths_ref[:, pl.ds(pl.multiple_of(x * GROUP, GROUP), GROUP)])
    l = lax.broadcasted_iota(jnp.int32, (256, 256), 0)
    m = lax.broadcasted_iota(jnp.int32, (256, 256), 1)
    other = jnp.bitwise_xor(jnp.bitwise_and(l >> 5, 1), core)
    sort = (m == other * 128 + (l >> 6) * 32 + jnp.bitwise_and(l, 31)).astype(bf16)

    def block(index):
        index = lax.rem(index + 4 * NY, NY)
        cols = grad_ref[0, :, pl.ds(pl.multiple_of(index * YB, YB), YB)]
        rows = _dot(sel, cols).astype(bf16)
        first = _dot(rows[:, :256], sort).astype(bf16)
        second = _dot(rows[:, 256:], sort).astype(bf16)
        mine = jnp.concatenate([first[:, :128], second[:, :128]], axis=1)
        others = jnp.concatenate([first[:, 128:], second[:, 128:]], axis=1)
        return mine, others

    def put(ref, j, value):
        ref[:, j * HALF : (j + 1) * HALF] = value

    for h, j in ((0, 0), (NY // 2, 7)):
        mine, others = block(y - h)
        put(keep_ref, j, mine)
        put(send_ref, j, others)
    for h in range(1, NY // 2):
        mine, others = block(y - h * step)
        put(keep_ref, 2 * h - 1, mine)
        put(keep_ref, 2 * h, others)
        mine, others = block(y + h * step)
        put(send_ref, 2 * h - 1, others)
        put(send_ref, 2 * h, mine)


def _softmax_kernel(
    depths_ref, documents_ref, q_ref, k_ref, v_ref, qc_ref, kc_ref, vc_ref, probs_ref, attended_ref, sel_ref
):
    docs_col, docs_row, valid_col, valid_row = [], [], [], []
    for b in range(NX):
        at = slice(b * GROUP, (b + 1) * GROUP)
        to = slice(b * CAP, (b + 1) * CAP)
        sel = _selection(depths_ref[:, at])
        sel_ref[to, :] = sel
        for src, dst in ((q_ref, qc_ref), (k_ref, kc_ref), (v_ref, vc_ref)):
            dst[to, :] = _dot(sel, src[0, at, :]).astype(bf16)
        docs = documents_ref[:, at].astype(f32)
        docs8 = jnp.broadcast_to(docs, (8, GROUP)).astype(bf16)
        ones8 = jnp.ones((8, GROUP), bf16)
        picked = sel.astype(f32)
        docs_col.append(jnp.sum(picked * docs, axis=1, keepdims=True))
        valid_col.append(jnp.sum(picked, axis=1, keepdims=True))
        docs_row.append(_dot(docs8, sel, NT)[0:1])
        valid_row.append(_dot(ones8, sel, NT)[0:1])
    doc_c = jnp.concatenate(docs_col, axis=0)
    doc_r = jnp.concatenate(docs_row, axis=1)
    val_c = jnp.concatenate(valid_col, axis=0)
    val_r = jnp.concatenate(valid_row, axis=1)
    doc_c = jnp.where(val_c > 0.5, doc_c, -1.0)
    doc_r = jnp.where(val_r > 0.5, doc_r, -2.0)
    i = lax.broadcasted_iota(jnp.int32, (ROWS, ROWS), 0)
    j = lax.broadcasted_iota(jnp.int32, (ROWS, ROWS), 1)
    allowed = (doc_c == doc_r) & (j <= i)
    scale = HD ** (-0.5)
    for h in range(HEADS):
        cols = slice(h * HD, (h + 1) * HD)
        scores = _dot(qc_ref[:, cols], kc_ref[:, cols], NT) * scale
        masked = jnp.where(allowed, scores, -1e30)
        top = jnp.max(masked, axis=1, keepdims=True)
        raw = jnp.where(allowed, jnp.exp(masked - top), 0.0)
        total = jnp.sum(raw, axis=1, keepdims=True)
        total = jnp.where(total > 0.0, total, 1.0)
        probs = raw * (1.0 / total)
        probs_ref[h] = probs
        attended_ref[:, cols] = _dot(probs.astype(bf16), vc_ref[:, cols])


def _project_kernel(
    own_ref, hop1_ref, hop2_ref, hop3_ref, hop4_ref, g0_ref, g1_ref, g3_ref, g2a_ref, g2b_ref, mine_ref, other_ref
):
    x = lax.axis_index("seq")

    def rows_at(shift):
        return pl.ds(pl.multiple_of(lax.rem(x + shift + NX, NX) * CAP, CAP), CAP)

    pieces = (
        (g0_ref, slice(0, CAP), mine_ref, 0),
        (g0_ref, slice(CAP, 2 * CAP), other_ref, 0),
        (g1_ref, slice(0, CAP), mine_ref, -1),
        (g1_ref, slice(CAP, 2 * CAP), other_ref, -1),
        (g3_ref, slice(0, CAP), mine_ref, 1),
        (g3_ref, slice(CAP, 2 * CAP), other_ref, 1),
        (g2a_ref, slice(0, CAP), mine_ref, 2),
        (g2b_ref, slice(0, CAP), other_ref, 2),
    )
    weights = (
        (own_ref, 0, HALF),
        (hop1_ref, HALF, 2 * HALF),
        (hop2_ref, 3 * HALF, 2 * HALF),
        (hop3_ref, 5 * HALF, 2 * HALF),
        (hop4_ref, 7 * HALF, HALF),
    )
    rows = jnp.concatenate([g[at, :] for g, at, _, _ in pieces], axis=0)
    total = None
    for w, k, n in weights:
        term = _dot(rows[:, k : k + n], w[...])
        total = term if total is None else total + term
    for n, (_, _, out, shift) in enumerate(pieces):
        out[rows_at(shift), :] = total[n * CAP : (n + 1) * CAP]


def _gradients_kernel(
    mine_ref, other_ref, qc_ref, kc_ref, vc_ref, probs_ref, attended_ref, sel_ref, dq_ref, dk_ref, dv_ref
):
    scale = HD ** (-0.5)
    for h in range(HEADS):
        cols = slice(h * HD, (h + 1) * HD)
        out_grad = (mine_ref[:, cols] + other_ref[:, cols]).astype(bf16)
        q, k, v = qc_ref[:, cols], kc_ref[:, cols], vc_ref[:, cols]
        probs = probs_ref[h]
        delta = jnp.sum(out_grad.astype(f32) * attended_ref[:, cols], axis=1, keepdims=True)
        dscore = (probs * (_dot(out_grad, v, NT) - delta)).astype(bf16)
        dv = _dot(probs.astype(bf16), out_grad, TN).astype(bf16)
        dq = (_dot(dscore, k) * scale).astype(bf16)
        dk = (_dot(dscore, q, TN) * scale).astype(bf16)
        for b in range(NX):
            at = slice(b * GROUP, (b + 1) * GROUP)
            frm = slice(b * CAP, (b + 1) * CAP)
            sel = sel_ref[frm, :]
            for src, dst in ((dq, dq_ref), (dk, dk_ref), (dv, dv_ref)):
                dst[0, at, cols] = _dot(sel, src[frm, :], TN).astype(bf16)


def _call(kernel, outs, flops, nbytes, exps=0):
    return pl.pallas_call(
        kernel,
        out_shape=tuple(jax.ShapeDtypeStruct(s, t) for s, t in outs),
        compiler_params=pltpu.CompilerParams(vmem_limit_bytes=VMEM),
        cost_estimate=pl.CostEstimate(flops=flops, bytes_accessed=nbytes, transcendentals=exps),
    )


def on_device(queries, key_states, value_states, grad_out, out_weight, depths, documents):
    copies = jnp.broadcast_to(out_weight[None], (NZ,) + out_weight.shape)
    own = lax.all_to_all(copies, "dp", 0, 0, axis_index_groups=Z_GROUPS).reshape(HALF, COLS)
    keep, send = _call(
        _cotangent_kernel, [((CAP, KC), bf16)] * 2, 2 * CAP * D * (GROUP + 256), 2 << 20
    )(depths, grad_out)
    got = lax.ppermute(send, "dp", SWAP)
    g0 = jnp.concatenate([keep, got], axis=0)
    g1 = lax.ppermute(g0, "seq", UP)
    g3 = lax.ppermute(g0, "seq", DOWN)
    g2a = lax.ppermute(g1[:CAP], "seq", UP)
    g2b = lax.ppermute(g3[CAP:], "seq", DOWN)
    hop1 = jnp.concatenate([lax.ppermute(own, "dp", ALONG), lax.ppermute(own, "dp", CROSS)], axis=0)
    hop2 = lax.ppermute(hop1, "dp", ALONG)
    hop3 = lax.ppermute(hop2, "dp", ALONG)
    hop4 = lax.ppermute(hop3[:HALF], "dp", ALONG)
    qc, kc, vc, probs, attended, sel = _call(
        _softmax_kernel,
        [((ROWS, COLS), bf16)] * 3
        + [((HEADS, ROWS, ROWS), f32), ((ROWS, COLS), f32), ((ROWS, GROUP), bf16)],
        4 * HEADS * ROWS * ROWS * HD,
        4 << 20,
        HEADS * ROWS * ROWS,
    )(depths, documents, queries, key_states, value_states)
    mine, other = _call(
        _project_kernel, [((ROWS, COLS), f32)] * 2, 4 * ROWS * KC * COLS, 5 << 20
    )(own, hop1, hop2, hop3, hop4, g0, g1, g3, g2a, g2b)
    theirs = lax.ppermute(other, "dp", SWAP)
    return _call(
        _gradients_kernel, [((1, SEQ, COLS), bf16)] * 3, 10 * HEADS * ROWS * ROWS * HD, 5 << 20
    )(mine, theirs, qc, kc, vc, probs, attended, sel)


def solution(mesh):
    return jax.shard_map(
        on_device,
        mesh=mesh,
        in_specs=(
            P("dp", None, "seq"),
            P("dp", None, "seq"),
            P("dp", None, "seq"),
            P("dp", "seq", None),
            P("dp", "seq"),
            P("dp", None),
            P("dp", None),
        ),
        out_specs=(P("dp", None, "seq"), P("dp", None, "seq"), P("dp", None, "seq")),
        check_vma=False,
    )
```

time: 180 us -> 87.7 us (0.49)
  waiting for transfers between devices: 142 us -> 13.8 us
  starting transfers between devices: 0.08 us -> 42 us
  blocking collectives: 0 us -> 21 us
  between operations: 14.2 us -> 0.91 us
  matrix products: 13.2 us -> 0 us
  Pallas kernels: 0 us -> 7.92 us
  local copies, waits for them, and re-layouts: 8.75 us -> 1.03 us
    all_gather x2 -> x0, waiting for transfers between devices: 141 us -> none  [the longest x1 88.6 us: project_rows(): lax.all_gather(out_weight, 'dp', axis=0, tiled=True)]
    ppermute x0 -> x11, starting transfers between devices: none -> 42 us  [the longest x1 5.32 us: on_device(): g2b = lax.ppermute(g3[CAP:], 'seq', DOWN)]
    all_to_all x0 -> x1, blocking collectives: none -> 21 us  [on_device(): lax.all_to_all(copies, 'dp', 0, 0, axis_index_groups=Z_GROUPS)]
    ppermute x0 -> x11, waiting for transfers between devices: none -> 13.8 us  [the longest x1 4.8 us: on_device(): g3 = lax.ppermute(g0, 'seq', DOWN)]
    dot_general x7 -> x0, matrix products: 13.2 us -> none  [the longest x1 5.97 us: project_rows(): jnp.dot(cotangent_rows, lax.all_gather(out_weight, 'dp', axis=0, tiled=Tr...]
    pallas_call x0 -> x4, Pallas kernels: none -> 7.92 us  [the longest x1 3.22 us: on_device(): _call(_gradients_kernel, [((1, SEQ, COLS), bf16)] * 3, 10 * HEADS * ROWS...]
    unnamed x11 -> x14, local copies, waits for them, and re-layouts: 4.98 us -> 0.07 us
    another operation x3 -> x0, local copies, waits for them, and re-layouts: 3.76 us -> none  [the longest x1 1.26 us: head_grads(): key_h = key_states.reshape(row_count, head_count, HD)]
  transfers between devices with their start and end apart: 2 -> 11, of which waited for: 2 -> 4; matrix products, arithmetic and copies ran while one was open for 3% -> 0% of each run, Pallas kernels for 0% -> 4%
where the time goes in v1:
time: 87.7 us; the launch traced here: 86.7 us
  starting transfers between devices  42 us (48%)
  blocking collectives  21 us (24%)
  waiting for transfers between devices  13.8 us (16%)
  Pallas kernels  7.92 us (9%)
  local copies, waits for them, and re-layouts  1.03 us (1%)
  between operations  0.91 us (1%)
    all_to_all x1, blocking collectives, on_device(): lax.all_to_all(copies, 'dp', 0, 0, axis_index_groups=Z_GROUPS)  21 us
    ppermute x1, starting transfers between devices, on_device(): g2b = lax.ppermute(g3[CAP:], 'seq', DOWN)  5.32 us
    ppermute x1, starting transfers between devices, on_device(): theirs = lax.ppermute(other, 'dp', SWAP)  5.1 us
    ppermute x1, starting transfers between devices, on_device(): lax.ppermute(own, 'dp', ALONG)  5.09 us
    ppermute x1, waiting for transfers between devices, on_device(): g3 = lax.ppermute(g0, 'seq', DOWN)  4.8 us
    ppermute x1, starting transfers between devices, on_device(): hop3 = lax.ppermute(hop2, 'dp', ALONG)  4.41 us
    ppermute x1, starting transfers between devices, on_device(): g3 = lax.ppermute(g0, 'seq', DOWN)  4.39 us
    ppermute x1, starting transfers between devices, on_device(): hop4 = lax.ppermute(hop3[:HALF], 'dp', ALONG)  4.3 us
  transfers between devices with their start and end apart: 11, of which 4 were waited for; matrix products, arithmetic and copies ran while one was open for 0% of the time, Pallas kernels for 4%

profile of v1, /device:TPU:1, one launch (start us, length us, event | category | flops | bytes accessed | tf_op | source)
XLA Modules:
  0.0 86.7 jit_solution(641697694370379248)
XLA Ops:
  0.6 0.0 copy-start
  0.6 0.9 broadcast_in_dim.2
  1.5 21.0 %all_to_all.5 = bf16[8,32,512]{2,1,0:T(8,128)(2,1)S(1)} all-to-all(bf16[8,32,512]{2,1,0:T(8,128)(2,1)S(1)} %broadcast_in_dim.2), channel_id=1, replica_groups={{0,8,16,24,32,40,48,56},{4,12,20,28,36,44,52,60},{64,72,80,88,96,104,11..., dimensions={0} | all-to-all | bytes 524288 | tf_op jit(solution)/shard_map/all_to_all | solution.py:206
  22.5 5.1 %collective-permute-start = (bf16[256,512]{1,0:T(8,128)(2,1)S(1)}, bf16[256,512]{1,0:T(8,128)(2,1)S(1)}, u32[]{:S(2)}, u32[]{:S(2)}) collective-permute-start(bf16[256,512]{1,0:T(8,128)(2,1)S(1)} %bitcast.1), channel_id=1, source_target_pairs={{0,64},{4,452},{8,72},{12,460},{16,80},{20,468},{24,88},{28,476},{... | collective-permute-start | bytes 786440 | tf_op jit(solution)/shard_map/ppermute | solution.py:216
  27.6 3.9 %collective-permute-start.1 = (bf16[256,512]{1,0:T(8,128)(2,1)S(1)}, bf16[256,512]{1,0:T(8,128)(2,1)S(1)}, u32[]{:S(2)}, u32[]{:S(2)}) collective-permute-start(bf16[256,512]{1,0:T(8,128)(2,1)S(1)} %bitcast.2), channel_id=1, source_target_pairs={{0,452},{4,64},{8,460},{12,72},{16,468},{20,80},{24,476},{28,88},{... | collective-permute-start | bytes 786440 | tf_op jit(solution)/shard_map/ppermute | solution.py:216
  31.6 0.0 collective-permute-done
  31.6 0.0 copy-start.4
  31.6 4.3 %collective-permute-done.1 = bf16[256,512]{1,0:T(8,128)(2,1)S(1)} collective-permute-done((bf16[256,512]{1,0:T(8,128)(2,1)S(1)}, bf16[256,512]{1,0:T(8,128)(2,1)S(1)}, u32[]{:S(2)}, u32[]{:S(2)}) %collective-permute-start.1) | collective-permute-done | bytes 262176 | tf_op jit(solution)/shard_map/ppermute | solution.py:216
  35.9 3.6 %collective-permute-start.2 = (bf16[512,512]{1,0:T(8,128)(2,1)S(1)}, bf16[512,512]{1,0:T(8,128)(2,1)S(1)}, u32[]{:S(2)}, u32[]{:S(2)}) collective-permute-start(bf16[512,512]{1,0:T(8,128)(2,1)S(1)} %constant_dynamic-update-slice_fusion.hop1_ref), channel_id=1, source_target_pairs={{0,64},{4,452},{8,72},{12,460},{16,80},{20,468},{24,88},{28,476},{... | collective-permute-start | bytes 1572872 | tf_op jit(solution)/shard_map/ppermute | solution.py:217
  39.5 0.0 copy-done
  39.6 0.0 copy-done.4
  39.6 1.4 %shard_map.94 = (bf16[64,2048]{1,0:T(8,128)(2,1)S(1)}, bf16[64,2048]{1,0:T(8,128)(2,1)S(1)}) custom-call(s32[1,512]{1,0:T(1,128)S(1)} %copy-done.4, bf16[1,128,4096]{2,1,0:T(8,128)(2,1)S(1)} %copy-done), custom_call_target="tpu_custom_call" | custom-call | flops 201326592 | bytes 2097152 | tf_op jit(solution)/shard_map/pallas_call | solution.py:207
  41.0 2.1 %collective-permute-start.5 = (bf16[64,2048]{1,0:T(8,128)(2,1)S(1)}, bf16[64,2048]{1,0:T(8,128)(2,1)S(1)}, u32[]{:S(2)}, u32[]{:S(2)}) collective-permute-start(bf16[64,2048]{1,0:T(8,128)(2,1)S(1)} %get-tuple-element.14), channel_id=1, source_target_pairs={{0,4},{4,0},{8,12},{12,8},{16,20},{20,16},{24,28},{28,24},{32,36},... | collective-permute-start | bytes 786440 | tf_op jit(solution)/shard_map/ppermute | solution.py:210
  43.1 1.3 %collective-permute-done.5 = bf16[64,2048]{1,0:T(8,128)(2,1)S(1)} collective-permute-done((bf16[64,2048]{1,0:T(8,128)(2,1)S(1)}, bf16[64,2048]{1,0:T(8,128)(2,1)S(1)}, u32[]{:S(2)}, u32[]{:S(2)}) %collective-permute-start.5) | collective-permute-done | bytes 262176 | tf_op jit(solution)/shard_map/ppermute | solution.py:210
  44.4 4.4 %collective-permute-start.7 = (bf16[128,2048]{1,0:T(8,128)(2,1)S(1)}, bf16[128,2048]{1,0:T(8,128)(2,1)S(1)}, u32[]{:S(2)}, u32[]{:S(2)}) collective-permute-start(bf16[128,2048]{1,0:T(8,128)(2,1)S(1)} %constant_dynamic-update-slice_fusion.2.g0_ref), channel_id=1, source_target_pairs={{0,3},{1,0},{2,1},{3,2},{4,7},{5,4},{6,5},{7,6},{8,11},{9,8},{10,9... | collective-permute-start | bytes 1572872 | tf_op jit(solution)/shard_map/ppermute | solution.py:213
  48.8 1.9 %collective-permute-start.6 = (bf16[128,2048]{1,0:T(8,128)(2,1)S(1)}, bf16[128,2048]{1,0:T(8,128)(2,1)S(1)}, u32[]{:S(2)}, u32[]{:S(2)}) collective-permute-start(bf16[128,2048]{1,0:T(8,128)(2,1)S(1)} %constant_dynamic-update-slice_fusion.2.g0_ref), channel_id=1, source_target_pairs={{0,1},{1,2},{2,3},{3,0},{4,5},{5,6},{6,7},{7,4},{8,9},{9,10},{10,1... | collective-permute-start | bytes 1572872 | tf_op jit(solution)/shard_map/ppermute | solution.py:212
  50.8 0.0 collective-permute-done.2.hop2_ref
  50.8 4.4 %collective-permute-start.3 = (bf16[512,512]{1,0:T(8,128)(2,1)S(1)}, bf16[512,512]{1,0:T(8,128)(2,1)S(1)}, u32[]{:S(2)}, u32[]{:S(2)}) collective-permute-start(bf16[512,512]{1,0:T(8,128)(2,1)S(1)} %collective-permute-done.2.hop2_ref), channel_id=1, source_target_pairs={{0,64},{4,452},{8,72},{12,460},{16,80},{20,468},{24,88},{28,476},{... | collective-permute-start | bytes 1572872 | tf_op jit(solution)/shard_map/ppermute | solution.py:218
  55.2 4.8 %collective-permute-done.7.g3_ref = bf16[128,2048]{1,0:T(8,128)(2,1)S(1)} collective-permute-done((bf16[128,2048]{1,0:T(8,128)(2,1)S(1)}, bf16[128,2048]{1,0:T(8,128)(2,1)S(1)}, u32[]{:S(2)}, u32[]{:S(2)}) %collective-permute-start.7) | collective-permute-done | bytes 524320 | tf_op jit(solution)/shard_map/ppermute | solution.py:213
  60.0 5.3 %collective-permute-start.9 = (bf16[64,2048]{1,0:T(8,128)(2,1)S(1)}, bf16[64,2048]{1,0:T(8,128)(2,1)S(1)}, u32[]{:S(2)}, u32[]{:S(2)}) collective-permute-start(bf16[64,2048]{1,0:T(8,128)(2,1)S(1)} %slice.14), channel_id=1, source_target_pairs={{0,3},{1,0},{2,1},{3,2},{4,7},{5,4},{6,5},{7,6},{8,11},{9,8},{10,9... | collective-permute-start | bytes 786440 | tf_op jit(solution)/shard_map/ppermute | solution.py:215
  65.3 0.0 collective-permute-done.6.g1_ref
  65.4 1.9 %collective-permute-start.8 = (bf16[64,2048]{1,0:T(8,128)(2,1)S(1)}, bf16[64,2048]{1,0:T(8,128)(2,1)S(1)}, u32[]{:S(2)}, u32[]{:S(2)}) collective-permute-start(bf16[64,2048]{1,0:T(8,128)(2,1)S(1)} %slice.13), channel_id=1, source_target_pairs={{0,1},{1,2},{2,3},{3,0},{4,5},{5,6},{6,7},{7,4},{8,9},{9,10},{10,1... | collective-permute-start | bytes 786440 | tf_op jit(solution)/shard_map/ppermute | solution.py:214
  67.3 0.0 collective-permute-done.3.hop3_ref
  67.3 0.0 copy-start.1
  67.3 0.0 copy-start.2
  67.3 0.0 copy-start.3
  67.4 4.3 %collective-permute-start.4 = (bf16[256,512]{1,0:T(8,128)(2,1)S(1)}, bf16[256,512]{1,0:T(8,128)(2,1)S(1)}, u32[]{:S(2)}, u32[]{:S(2)}) collective-permute-start(bf16[256,512]{1,0:T(8,128)(2,1)S(1)} %slice.12), channel_id=1, source_target_pairs={{0,64},{4,452},{8,72},{12,460},{16,80},{20,468},{24,88},{28,476},{... | collective-permute-start | bytes 786440 | tf_op jit(solution)/shard_map/ppermute | solution.py:219
  71.7 0.0 collective-permute-done.9.g2b_ref
  71.7 3.3 %collective-permute-done.8.g2a_ref = bf16[64,2048]{1,0:T(8,128)(2,1)S(1)} collective-permute-done((bf16[64,2048]{1,0:T(8,128)(2,1)S(1)}, bf16[64,2048]{1,0:T(8,128)(2,1)S(1)}, u32[]{:S(2)}, u32[]{:S(2)}) %collective-permute-start.8) | collective-permute-done | bytes 262176 | tf_op jit(solution)/shard_map/ppermute | solution.py:214
  75.0 0.0 collective-permute-done.4.hop4_ref
  75.0 0.0 copy-start.5
  75.0 1.2 %shard_map.95 = (f32[256,512]{1,0:T(8,128)S(1)}, f32[256,512]{1,0:T(8,128)S(1)}) custom-call(bf16[256,512]{1,0:T(8,128)(2,1)S(1)} %bitcast.3, bf16[512,512]{1,0:T(8,128)(2,1)S(1)} %constant_dynamic-update-slice_fusion.hop1_ref, bf16[512,512]{1,0:T(8,128)(2,1)S(1)} %collective-permute-done.2.hop2_ref, bf16[512,512]{1,0:T(8,128)(2,1)S(1)} %collective-permute-done.3.hop3_ref, ...), custom_call_target="tpu_custom_call" | custom-call | flops 1073741824 | bytes 5242880 | tf_op jit(solution)/shard_map/pallas_call | solution.py:228
  76.3 5.1 %collective-permute-start.10 = (f32[256,512]{1,0:T(8,128)S(1)}, f32[256,512]{1,0:T(8,128)S(1)}, u32[]{:S(2)}, u32[]{:S(2)}) collective-permute-start(f32[256,512]{1,0:T(8,128)S(1)} %get-tuple-element.16), channel_id=1, source_target_pairs={{0,4},{4,0},{8,12},{12,8},{16,20},{20,16},{24,28},{28,24},{32,36},... | collective-permute-start | bytes 1572872 | tf_op jit(solution)/shard_map/ppermute | solution.py:231
  81.4 0.0 copy-done.1
  81.4 0.0 copy-done.2
  81.4 0.0 copy-done.3
  81.4 0.0 copy-done.5
  81.4 2.0 %shard_map.96 = (bf16[256,512]{1,0:T(8,128)(2,1)S(1)}, bf16[256,512]{1,0:T(8,128)(2,1)S(1)}, bf16[256,512]{1,0:T(8,128)(2,1)S(1)}, f32[4,256,256]{2,1,0:T(8,128)...) custom-call(s32[1,512]{1,0:T(1,128)S(1)} %copy-done.4, s32[1,512]{1,0:T(1,128)S(1)} %copy-done.5, ...), custom_call_target="tpu_custom_call" | custom-call | flops 134217728 | bytes 4194304 | tf_op jit(solution)/shard_map/pallas_call | solution.py:220
  83.5 0.0 collective-permute-done.10.other_ref
  83.5 3.2 %shard_map.97 = (bf16[1,512,512]{2,1,0:T(8,128)(2,1)}, bf16[1,512,512]{2,1,0:T(8,128)(2,1)}, bf16[1,512,512]{2,1,0:T(8,128)(2,1)}) custom-call(f32[256,512]{1,0:T(8,128)S(1)} %get-tuple-element.15.mine_ref, f32[256,512]{1,0:T(8,128)S(1)} %collective-permute-done.10.other_ref, bf16[256,512]{1,0:T(8,128)(2,1)S(1)} %get-tuple-element.17.qc_ref, ...), custom_call_target="tpu_custom_call" | custom-call | flops 335544320 | bytes 5242880 | tf_op jit(solution)/shard_map/pallas_call | solution.py:232
  (7 shorter events, 0.1 us)
Async XLA Ops:
  0.6 38.9 %copy-start = (bf16[1,128,4096]{2,1,0:T(8,128)(2,1)S(1)}, bf16[1,128,4096]{2,1,0:T(8,128)(2,1)}, u32[]{:S(2)}) copy-start(bf16[1,128,4096]{2,1,0:T(8,128)(2,1)} %grad_ref.1) | copy-start | bytes 3145732
  22.5 9.0 %collective-permute-start = (bf16[256,512]{1,0:T(8,128)(2,1)S(1)}, bf16[256,512]{1,0:T(8,128)(2,1)S(1)}, u32[]{:S(2)}, u32[]{:S(2)}) collective-permute-start(bf16[256,512]{1,0:T(8,128)(2,1)S(1)} %bitcast.1), channel_id=1, source_target_pairs={{0,64},{4,452},{8,72},{12,460},{16,80},{20,468},{24,88},{28,476},{... | collective-permute-start | bytes 786440 | tf_op jit(solution)/shard_map/ppermute | solution.py:216
  27.6 8.3 %collective-permute-start.1 = (bf16[256,512]{1,0:T(8,128)(2,1)S(1)}, bf16[256,512]{1,0:T(8,128)(2,1)S(1)}, u32[]{:S(2)}, u32[]{:S(2)}) collective-permute-start(bf16[256,512]{1,0:T(8,128)(2,1)S(1)} %bitcast.2), channel_id=1, source_target_pairs={{0,452},{4,64},{8,460},{12,72},{16,468},{20,80},{24,476},{28,88},{... | collective-permute-start | bytes 786440 | tf_op jit(solution)/shard_map/ppermute | solution.py:216
  31.6 7.9 %copy-start.4 = (s32[1,512]{1,0:T(1,128)S(1)}, s32[1,512]{1,0:T(1,128)}, u32[]{:S(2)}) copy-start(s32[1,512]{1,0:T(1,128)} %depths_ref.3) | copy-start | bytes 6148
  35.9 14.8 %collective-permute-start.2 = (bf16[512,512]{1,0:T(8,128)(2,1)S(1)}, bf16[512,512]{1,0:T(8,128)(2,1)S(1)}, u32[]{:S(2)}, u32[]{:S(2)}) collective-permute-start(bf16[512,512]{1,0:T(8,128)(2,1)S(1)} %constant_dynamic-update-slice_fusion.hop1_ref), channel_id=1, source_target_pairs={{0,64},{4,452},{8,72},{12,460},{16,80},{20,468},{24,88},{28,476},{... | collective-permute-start | bytes 1572872 | tf_op jit(solution)/shard_map/ppermute | solution.py:217
  41.0 3.4 %collective-permute-start.5 = (bf16[64,2048]{1,0:T(8,128)(2,1)S(1)}, bf16[64,2048]{1,0:T(8,128)(2,1)S(1)}, u32[]{:S(2)}, u32[]{:S(2)}) collective-permute-start(bf16[64,2048]{1,0:T(8,128)(2,1)S(1)} %get-tuple-element.14), channel_id=1, source_target_pairs={{0,4},{4,0},{8,12},{12,8},{16,20},{20,16},{24,28},{28,24},{32,36},... | collective-permute-start | bytes 786440 | tf_op jit(solution)/shard_map/ppermute | solution.py:210
  44.4 15.5 %collective-permute-start.7 = (bf16[128,2048]{1,0:T(8,128)(2,1)S(1)}, bf16[128,2048]{1,0:T(8,128)(2,1)S(1)}, u32[]{:S(2)}, u32[]{:S(2)}) collective-permute-start(bf16[128,2048]{1,0:T(8,128)(2,1)S(1)} %constant_dynamic-update-slice_fusion.2.g0_ref), channel_id=1, source_target_pairs={{0,3},{1,0},{2,1},{3,2},{4,7},{5,4},{6,5},{7,6},{8,11},{9,8},{10,9... | collective-permute-start | bytes 1572872 | tf_op jit(solution)/shard_map/ppermute | solution.py:213
  48.8 16.5 %collective-permute-start.6 = (bf16[128,2048]{1,0:T(8,128)(2,1)S(1)}, bf16[128,2048]{1,0:T(8,128)(2,1)S(1)}, u32[]{:S(2)}, u32[]{:S(2)}) collective-permute-start(bf16[128,2048]{1,0:T(8,128)(2,1)S(1)} %constant_dynamic-update-slice_fusion.2.g0_ref), channel_id=1, source_target_pairs={{0,1},{1,2},{2,3},{3,0},{4,5},{5,6},{6,7},{7,4},{8,9},{9,10},{10,1... | collective-permute-start | bytes 1572872 | tf_op jit(solution)/shard_map/ppermute | solution.py:212
  50.8 16.5 %collective-permute-start.3 = (bf16[512,512]{1,0:T(8,128)(2,1)S(1)}, bf16[512,512]{1,0:T(8,128)(2,1)S(1)}, u32[]{:S(2)}, u32[]{:S(2)}) collective-permute-start(bf16[512,512]{1,0:T(8,128)(2,1)S(1)} %collective-permute-done.2.hop2_ref), channel_id=1, source_target_pairs={{0,64},{4,452},{8,72},{12,460},{16,80},{20,468},{24,88},{28,476},{... | collective-permute-start | bytes 1572872 | tf_op jit(solution)/shard_map/ppermute | solution.py:218
  60.0 11.7 %collective-permute-start.9 = (bf16[64,2048]{1,0:T(8,128)(2,1)S(1)}, bf16[64,2048]{1,0:T(8,128)(2,1)S(1)}, u32[]{:S(2)}, u32[]{:S(2)}) collective-permute-start(bf16[64,2048]{1,0:T(8,128)(2,1)S(1)} %slice.14), channel_id=1, source_target_pairs={{0,3},{1,0},{2,1},{3,2},{4,7},{5,4},{6,5},{7,6},{8,11},{9,8},{10,9... | collective-permute-start | bytes 786440 | tf_op jit(solution)/shard_map/ppermute | solution.py:215
  65.4 9.7 %collective-permute-start.8 = (bf16[64,2048]{1,0:T(8,128)(2,1)S(1)}, bf16[64,2048]{1,0:T(8,128)(2,1)S(1)}, u32[]{:S(2)}, u32[]{:S(2)}) collective-permute-start(bf16[64,2048]{1,0:T(8,128)(2,1)S(1)} %slice.13), channel_id=1, source_target_pairs={{0,1},{1,2},{2,3},{3,0},{4,5},{5,6},{6,7},{7,4},{8,9},{9,10},{10,1... | collective-permute-start | bytes 786440 | tf_op jit(solution)/shard_map/ppermute | solution.py:214
  67.3 14.1 %copy-start.1 = (bf16[1,512,512]{2,1,0:T(8,128)(2,1)S(1)}, bf16[1,512,512]{2,1,0:T(8,128)(2,1)}, u32[]{:S(2)}) copy-start(bf16[1,512,512]{2,1,0:T(8,128)(2,1)} %q_ref.1) | copy-start | bytes 1572868
  67.3 14.1 %copy-start.2 = (bf16[1,512,512]{2,1,0:T(8,128)(2,1)S(1)}, bf16[1,512,512]{2,1,0:T(8,128)(2,1)}, u32[]{:S(2)}) copy-start(bf16[1,512,512]{2,1,0:T(8,128)(2,1)} %k_ref.1) | copy-start | bytes 1572868
  67.3 14.1 %copy-start.3 = (bf16[1,512,512]{2,1,0:T(8,128)(2,1)S(1)}, bf16[1,512,512]{2,1,0:T(8,128)(2,1)}, u32[]{:S(2)}) copy-start(bf16[1,512,512]{2,1,0:T(8,128)(2,1)} %v_ref.1) | copy-start | bytes 1572868
  67.4 7.7 %collective-permute-start.4 = (bf16[256,512]{1,0:T(8,128)(2,1)S(1)}, bf16[256,512]{1,0:T(8,128)(2,1)S(1)}, u32[]{:S(2)}, u32[]{:S(2)}) collective-permute-start(bf16[256,512]{1,0:T(8,128)(2,1)S(1)} %slice.12), channel_id=1, source_target_pairs={{0,64},{4,452},{8,72},{12,460},{16,80},{20,468},{24,88},{28,476},{... | collective-permute-start | bytes 786440 | tf_op jit(solution)/shard_map/ppermute | solution.py:219
  75.0 6.4 %copy-start.5 = (s32[1,512]{1,0:T(1,128)S(1)}, s32[1,512]{1,0:T(1,128)}, u32[]{:S(2)}) copy-start(s32[1,512]{1,0:T(1,128)} %documents_ref.1) | copy-start | bytes 6148
  76.3 7.2 %collective-permute-start.10 = (f32[256,512]{1,0:T(8,128)S(1)}, f32[256,512]{1,0:T(8,128)S(1)}, u32[]{:S(2)}, u32[]{:S(2)}) collective-permute-start(f32[256,512]{1,0:T(8,128)S(1)} %get-tuple-element.16), channel_id=1, source_target_pairs={{0,4},{4,0},{8,12},{12,8},{16,20},{20,16},{24,28},{28,24},{32,36},... | collective-permute-start | bytes 1572872 | tf_op jit(solution)/shard_map/ppermute | solution.py:231

commit v2 on v1

--- a/solution.py
+++ b/solution.py
@@ -33,10 +33,19 @@
 _ALL = [(y, z, c) for y in range(NY) for z in range(NZ) for c in range(2)]
 Z_GROUPS = [[_place(y, z, c) for z in range(NZ)] for y in range(NY) for c in range(2)]
 SWAP = [(_place(y, z, c), _place(y, z, 1 - c)) for y, z, c in _ALL]
-ALONG = [(_place(y, z, c), _place(y + 1 - 2 * c, z, c)) for y, z, c in _ALL]
-CROSS = [(_place(y, z, c), _place(y + 2 * c - 1, z, 1 - c)) for y, z, c in _ALL]
-UP = [(i, (i + 1) % NX) for i in range(NX)]
-DOWN = [(i, (i + NX - 1) % NX) for i in range(NX)]
+Y_FIRST = [
+    (_place(y, z, c), _place(y + 1 - 2 * (c ^ (z & 1)), z, c ^ (z & 1))) for y, z, c in _ALL
+]
+Y_ALONG = [(_place(y, z, c), _place(y + 1 - 2 * c, z, c)) for y, z, c in _ALL]
+Z_SWAP = [(_place(y, z, c), _place(y, z ^ 1, c)) for y, z, c in _ALL]
+X_ALONG, X_AGAINST = (
+    [
+        (_place(y, z, c) * NX + x, _place(y, z, c) * NX + (x + way * (1 - 2 * c)) % NX)
+        for y, z, c in _ALL
+        for x in range(NX)
+    ]
+    for way in (1, -1)
+)
 
 
 def _dot(a, b, dims=(((1,), (0,)), ((), ()))):
@@ -56,42 +65,42 @@
     return (slot == rank).astype(bf16)
 
 
-def _cotangent_kernel(depths_ref, grad_ref, keep_ref, send_ref):
+def _cotangent_kernel(depths_ref, grad_ref, keep_ref, send_ref, q_ref, o_ref):
     dp = lax.axis_index("dp")
     x = lax.axis_index("seq")
     core = lax.rem(dp, 2)
+    odd = lax.rem(lax.div(dp, 2), 2)
     y = lax.div(dp, 2 * NZ)
     step = 1 - 2 * core
     sel = _selection(depths_ref[:, pl.ds(pl.multiple_of(x * GROUP, GROUP), GROUP)])
     l = lax.broadcasted_iota(jnp.int32, (256, 256), 0)
     m = lax.broadcasted_iota(jnp.int32, (256, 256), 1)
-    other = jnp.bitwise_xor(jnp.bitwise_and(l >> 5, 1), core)
+    other = jnp.bitwise_xor(jnp.bitwise_and(l >> 5, 1), jnp.bitwise_xor(core, odd))
     sort = (m == other * 128 + (l >> 6) * 32 + jnp.bitwise_and(l, 31)).astype(bf16)
-
-    def block(index):
+    rows = _dot(sel, grad_ref[0]).astype(bf16)
+    for n in range(D // 256):
+        at = slice(n * 128, (n + 1) * 128)
+        pair = _dot(rows[:, n * 256 : (n + 1) * 256], sort).astype(bf16)
+        q_ref[:, at] = pair[:, :128]
+        o_ref[:, at] = pair[:, 128:]
+
+    def block(ref, index):
         index = lax.rem(index + 4 * NY, NY)
-        cols = grad_ref[0, :, pl.ds(pl.multiple_of(index * YB, YB), YB)]
-        rows = _dot(sel, cols).astype(bf16)
-        first = _dot(rows[:, :256], sort).astype(bf16)
-        second = _dot(rows[:, 256:], sort).astype(bf16)
-        mine = jnp.concatenate([first[:, :128], second[:, :128]], axis=1)
-        others = jnp.concatenate([first[:, 128:], second[:, 128:]], axis=1)
-        return mine, others
+        return ref[:, pl.ds(pl.multiple_of(index * HALF, HALF), HALF)]
 
     def put(ref, j, value):
         ref[:, j * HALF : (j + 1) * HALF] = value
 
-    for h, j in ((0, 0), (NY // 2, 7)):
-        mine, others = block(y - h)
-        put(keep_ref, j, mine)
-        put(send_ref, j, others)
+    own_q, own_o = block(q_ref, y), block(o_ref, y)
+    put(keep_ref, 0, jnp.where(odd == 0, own_q, own_o))
+    put(send_ref, 0, jnp.where(odd == 0, own_o, own_q))
+    put(keep_ref, 7, block(q_ref, y + NY // 2))
+    put(send_ref, 7, block(o_ref, y + NY // 2))
     for h in range(1, NY // 2):
-        mine, others = block(y - h * step)
-        put(keep_ref, 2 * h - 1, mine)
-        put(keep_ref, 2 * h, others)
-        mine, others = block(y + h * step)
-        put(send_ref, 2 * h - 1, others)
-        put(send_ref, 2 * h, mine)
+        put(keep_ref, 2 * h - 1, block(q_ref, y - h * step))
+        put(keep_ref, 2 * h, block(o_ref, y - h * step))
+        put(send_ref, 2 * h - 1, block(o_ref, y + h * step))
+        put(send_ref, 2 * h, block(q_ref, y + h * step))
 
 
 def _softmax_kernel(
@@ -136,38 +145,33 @@
         attended_ref[:, cols] = _dot(probs.astype(bf16), vc_ref[:, cols])
 
 
-def _project_kernel(
-    own_ref, hop1_ref, hop2_ref, hop3_ref, hop4_ref, g0_ref, g1_ref, g3_ref, g2a_ref, g2b_ref, mine_ref, other_ref
+def _partial(g_refs, w_refs, start):
+    total = None
+    for n, w_ref in enumerate(w_refs):
+        cols = slice(start + n * HALF, start + (n + 1) * HALF)
+        term = _dot(jnp.concatenate([g[:, cols] for g in g_refs], axis=0), w_ref[...])
+        total = term if total is None else total + term
+    return total
+
+
+def _project_first_kernel(own_ref, a1_ref, b1_ref, a2_ref, b2_ref, g0_ref, g1_ref, g2_ref, g3_ref, out_ref):
+    out_ref[...] = _partial(
+        (g0_ref, g1_ref, g2_ref, g3_ref), (own_ref, a1_ref, b1_ref, a2_ref, b2_ref), 0
+    )
+
+
+def _project_last_kernel(
+    first_ref, a3_ref, b3_ref, a4_ref, g0_ref, g1_ref, g2_ref, g3_ref, mine_ref, other_ref
 ):
     x = lax.axis_index("seq")
-
-    def rows_at(shift):
-        return pl.ds(pl.multiple_of(lax.rem(x + shift + NX, NX) * CAP, CAP), CAP)
-
-    pieces = (
-        (g0_ref, slice(0, CAP), mine_ref, 0),
-        (g0_ref, slice(CAP, 2 * CAP), other_ref, 0),
-        (g1_ref, slice(0, CAP), mine_ref, -1),
-        (g1_ref, slice(CAP, 2 * CAP), other_ref, -1),
-        (g3_ref, slice(0, CAP), mine_ref, 1),
-        (g3_ref, slice(CAP, 2 * CAP), other_ref, 1),
-        (g2a_ref, slice(0, CAP), mine_ref, 2),
-        (g2b_ref, slice(0, CAP), other_ref, 2),
-    )
-    weights = (
-        (own_ref, 0, HALF),
-        (hop1_ref, HALF, 2 * HALF),
-        (hop2_ref, 3 * HALF, 2 * HALF),
-        (hop3_ref, 5 * HALF, 2 * HALF),
-        (hop4_ref, 7 * HALF, HALF),
-    )
-    rows = jnp.concatenate([g[at, :] for g, at, _, _ in pieces], axis=0)
-    total = None
-    for w, k, n in weights:
-        term = _dot(rows[:, k : k + n], w[...])
-        total = term if total is None else total + term
-    for n, (_, _, out, shift) in enumerate(pieces):
-        out[rows_at(shift), :] = total[n * CAP : (n + 1) * CAP]
+    step = 1 - 2 * lax.rem(lax.axis_index("dp"), 2)
+    total = first_ref[...] + _partial(
+        (g0_ref, g1_ref, g2_ref, g3_ref), (a3_ref, b3_ref, a4_ref), 5 * HALF
+    )
+    for n, shift in enumerate((0, -step, 2, step)):
+        at = pl.ds(pl.multiple_of(lax.rem(x + shift + NX, NX) * CAP, CAP), CAP)
+        mine_ref[at, :] = total[2 * n * CAP : (2 * n + 1) * CAP]
+        other_ref[at, :] = total[(2 * n + 1) * CAP : (2 * n + 2) * CAP]
 
 
 def _gradients_kernel(
@@ -192,31 +196,41 @@
                 dst[0, at, cols] = _dot(sel, src[frm, :], TN).astype(bf16)
 
 
-def _call(kernel, outs, flops, nbytes, exps=0):
+def _call(kernel, outs, flops, nbytes, exps=0, scratch=()):
     return pl.pallas_call(
         kernel,
         out_shape=tuple(jax.ShapeDtypeStruct(s, t) for s, t in outs),
+        scratch_shapes=scratch,
         compiler_params=pltpu.CompilerParams(vmem_limit_bytes=VMEM),
         cost_estimate=pl.CostEstimate(flops=flops, bytes_accessed=nbytes, transcendentals=exps),
     )
 
 
 def on_device(queries, key_states, value_states, grad_out, out_weight, depths, documents):
-    copies = jnp.broadcast_to(out_weight[None], (NZ,) + out_weight.shape)
-    own = lax.all_to_all(copies, "dp", 0, 0, axis_index_groups=Z_GROUPS).reshape(HALF, COLS)
     keep, send = _call(
-        _cotangent_kernel, [((CAP, KC), bf16)] * 2, 2 * CAP * D * (GROUP + 256), 2 << 20
+        _cotangent_kernel,
+        [((CAP, KC), bf16)] * 2,
+        2 * CAP * D * (GROUP + 256),
+        2 << 20,
+        scratch=[pltpu.VMEM((CAP, KC), bf16)] * 2,
     )(depths, grad_out)
     got = lax.ppermute(send, "dp", SWAP)
     g0 = jnp.concatenate([keep, got], axis=0)
-    g1 = lax.ppermute(g0, "seq", UP)
-    g3 = lax.ppermute(g0, "seq", DOWN)
-    g2a = lax.ppermute(g1[:CAP], "seq", UP)
-    g2b = lax.ppermute(g3[CAP:], "seq", DOWN)
-    hop1 = jnp.concatenate([lax.ppermute(own, "dp", ALONG), lax.ppermute(own, "dp", CROSS)], axis=0)
-    hop2 = lax.ppermute(hop1, "dp", ALONG)
-    hop3 = lax.ppermute(hop2, "dp", ALONG)
-    hop4 = lax.ppermute(hop3[:HALF], "dp", ALONG)
+    copies = jnp.broadcast_to(out_weight[None], (NZ,) + out_weight.shape)
+    own = lax.all_to_all(copies, "dp", 0, 0, axis_index_groups=Z_GROUPS).reshape(HALF, COLS)
+    g1 = lax.ppermute(g0, ("dp", "seq"), X_ALONG)
+    g3 = lax.ppermute(g0, ("dp", "seq"), X_AGAINST)
+    g2 = lax.ppermute(g1, ("dp", "seq"), X_ALONG)
+    a1 = lax.ppermute(own, "dp", Y_FIRST)
+    a1, g1 = lax.optimization_barrier((a1, g1))
+    a2 = lax.ppermute(a1, "dp", Y_ALONG)
+    b1 = lax.ppermute(a1, "dp", Z_SWAP)
+    a2, g3 = lax.optimization_barrier((a2, g3))
+    a3 = lax.ppermute(a2, "dp", Y_ALONG)
+    b2 = lax.ppermute(a2, "dp", Z_SWAP)
+    a3, b1, g2 = lax.optimization_barrier((a3, b1, g2))
+    a4 = lax.ppermute(a3, "dp", Y_ALONG)
+    b3 = lax.ppermute(a3, "dp", Z_SWAP)
     qc, kc, vc, probs, attended, sel = _call(
         _softmax_kernel,
         [((ROWS, COLS), bf16)] * 3
@@ -225,9 +239,12 @@
         4 << 20,
         HEADS * ROWS * ROWS,
     )(depths, documents, queries, key_states, value_states)
+    first = _call(
+        _project_first_kernel, [((2 * ROWS, COLS), f32)], 20 * ROWS * HALF * COLS, 5 << 20
+    )(own, a1, b1, a2, b2, g0, g1, g2, g3)[0]
     mine, other = _call(
-        _project_kernel, [((ROWS, COLS), f32)] * 2, 4 * ROWS * KC * COLS, 5 << 20
-    )(own, hop1, hop2, hop3, hop4, g0, g1, g3, g2a, g2b)
+        _project_last_kernel, [((ROWS, COLS), f32)] * 2, 12 * ROWS * HALF * COLS, 5 << 20
+    )(first, a3, b3, a4, g0, g1, g2, g3)
     theirs = lax.ppermute(other, "dp", SWAP)
     return _call(
         _gradients_kernel, [((1, SEQ, COLS), bf16)] * 3, 10 * HEADS * ROWS * ROWS * HD, 5 << 20

time: 87.7 us -> 79.4 us (0.905)
  blocking collectives: 21 us -> 0 us
  starting transfers between devices: 42 us -> 52.2 us
  local copies, waits for them, and re-layouts: 1.03 us -> 2.69 us
  waiting for transfers between devices: 13.8 us -> 15.3 us
    all_to_all x1 -> x0, blocking collectives: 21 us -> none  [on_device(): lax.all_to_all(copies, 'dp', 0, 0, axis_index_groups=Z_GROUPS)]
    all_to_all x0 -> x1, waiting for transfers between devices: none -> 7.91 us  [on_device(): lax.all_to_all(copies, 'dp', 0, 0, axis_index_groups=Z_GROUPS)]
    ppermute x1, starting transfers between devices: 2.05 us -> 8.78 us  [on_device(): got = lax.ppermute(send, 'dp', SWAP)]
    ppermute x9 -> x10, waiting for transfers between devices: 12.4 us -> 7.35 us  [the longest x1 5.2 us: on_device(): b3 = lax.ppermute(a3, 'dp', Z_SWAP)]
    all_to_all x0 -> x1, starting transfers between devices: none -> 4.67 us  [on_device(): lax.all_to_all(copies, 'dp', 0, 0, axis_index_groups=Z_GROUPS)]
    ppermute x1, starting transfers between devices: 5.1 us -> 3.05 us  [on_device(): theirs = lax.ppermute(other, 'dp', SWAP)]
    unnamed x14 -> x17, local copies, waits for them, and re-layouts: 0.07 us -> 1.95 us
    ppermute x1, waiting for transfers between devices: 1.34 us -> 0.01 us  [on_device(): got = lax.ppermute(send, 'dp', SWAP)]
  transfers between devices with their start and end apart: 11 -> 13, of which waited for: 4 -> 5; matrix products, arithmetic and copies ran while one was open for 0% -> 1% of each run, Pallas kernels for 4% -> 4%
where the time goes in v2:
time: 79.4 us; the launch traced here: 78.6 us
  starting transfers between devices  52.2 us (66%)
  waiting for transfers between devices  15.3 us (19%)
  Pallas kernels  7.53 us (9%)
  local copies, waits for them, and re-layouts  2.69 us (3%)
  between operations  0.9 us (1%)
    ppermute x1, starting transfers between devices, on_device(): got = lax.ppermute(send, 'dp', SWAP)  8.78 us
    all_to_all x1, waiting for transfers between devices, on_device(): lax.all_to_all(copies, 'dp', 0, 0, axis_index_groups=Z_GROUPS)  7.91 us
    ppermute x1, waiting for transfers between devices, on_device(): b3 = lax.ppermute(a3, 'dp', Z_SWAP)  5.2 us
    ppermute x1, starting transfers between devices, on_device(): a1 = lax.ppermute(own, 'dp', Y_FIRST)  5.08 us
    ppermute x1, starting transfers between devices, on_device(): a2 = lax.ppermute(a1, 'dp', Y_ALONG)  5.01 us
    all_to_all x1, starting transfers between devices, on_device(): lax.all_to_all(copies, 'dp', 0, 0, axis_index_groups=Z_GROUPS)  4.67 us
    ppermute x1, starting transfers between devices, on_device(): g2 = lax.ppermute(g1, ('dp', 'seq'), X_ALONG)  4.4 us
    ppermute x1, starting transfers between devices, on_device(): g1 = lax.ppermute(g0, ('dp', 'seq'), X_ALONG)  4.39 us
  transfers between devices with their start and end apart: 13, of which 5 were waited for; matrix products, arithmetic and copies ran while one was open for 1% of the time, Pallas kernels for 4%

profile of v2, /device:TPU:1, one launch (start us, length us, event | category | flops | bytes accessed | tf_op | source)
XLA Modules:
  0.0 78.6 jit_solution(2958641586757254957)
XLA Ops:
  0.6 0.0 copy-start
  0.6 1.2 %copy-done = bf16[1,128,4096]{2,1,0:T(8,128)(2,1)S(1)} copy-done((bf16[1,128,4096]{2,1,0:T(8,128)(2,1)S(1)}, bf16[1,128,4096]{2,1,0:T(8,128)(2,1)}, u32[]{:S(2)}) %copy-start) | copy-done | bytes 1048600
  1.9 0.0 copy-start.4
  1.9 0.7 copy-done.4
  2.5 0.0 copy-start.7
  2.5 0.9 %shard_map.94 = (bf16[64,2048]{1,0:T(8,128)(2,1)S(1)}, bf16[64,2048]{1,0:T(8,128)(2,1)S(1)}) custom-call(s32[1,512]{1,0:T(1,128)S(1)} %copy-done.4, bf16[1,128,4096]{2,1,0:T(8,128)(2,1)S(1)} %copy-done), custom_call_target="tpu_custom_call" | custom-call | flops 201326592 | bytes 2097152 | tf_op jit(solution)/shard_map/pallas_call | solution.py:210
  3.4 8.8 %collective-permute-start.1 = (bf16[64,2048]{1,0:T(8,128)(2,1)S(1)}, bf16[64,2048]{1,0:T(8,128)(2,1)S(1)}, u32[]{:S(2)}, u32[]{:S(2)}) collective-permute-start(bf16[64,2048]{1,0:T(8,128)(2,1)S(1)} %get-tuple-element.21), channel_id=1, source_target_pairs={{0,4},{4,0},{8,12},{12,8},{16,20},{20,16},{24,28},{28,24},{32,36},... | collective-permute-start | bytes 786440 | tf_op jit(solution)/shard_map/ppermute | solution.py:217
  12.2 0.0 copy-done.7
  12.2 0.7 broadcast_in_dim.2
  12.9 4.7 %all-to-all-start = ((bf16[8,32,512]{2,1,0:T(8,128)(2,1)}), bf16[8,32,512]{2,1,0:T(8,128)(2,1)S(1)}, u32[]{:S(2)}, u32[]{:S(2)}) async-start(bf16[8,32,512]{2,1,0:T(8,128)(2,1)} %broadcast_in_dim.2), calls=%async_computation | async-start | bytes 524288 | tf_op jit(solution)/shard_map/all_to_all | solution.py:220
  17.6 0.0 collective-permute-done.1
  17.7 4.4 %collective-permute-start.2 = (bf16[128,2048]{1,0:T(8,128)(2,1)S(1)}, bf16[128,2048]{1,0:T(8,128)(2,1)S(1)}, u32[]{:S(2)}, u32[]{:S(2)}) collective-permute-start(bf16[128,2048]{1,0:T(8,128)(2,1)S(1)} %constant_dynamic-update-slice_fusion.g0_ref), channel_id=1, source_target_pairs={{0,1},{1,2},{2,3},{3,0},{4,7},{5,4},{6,5},{7,6},{8,9},{9,10},{10,1... | collective-permute-start | bytes 1572872 | tf_op jit(solution)/shard_map/ppermute | solution.py:221
  22.1 7.9 %all-to-all-done = bf16[8,32,512]{2,1,0:T(8,128)(2,1)S(1)} async-done(((bf16[8,32,512]{2,1,0:T(8,128)(2,1)}), bf16[8,32,512]{2,1,0:T(8,128)(2,1)S(1)}, u32[]{:S(2)}, u32[]{:S(2)}) %all-to-all-start) | async-done | bytes 262176 | tf_op jit(solution)/shard_map/all_to_all | solution.py:220
  30.0 5.1 %collective-permute-start = (bf16[256,512]{1,0:T(8,128)(2,1)S(1)}, bf16[256,512]{1,0:T(8,128)(2,1)S(1)}, u32[]{:S(2)}, u32[]{:S(2)}) collective-permute-start(bf16[256,512]{1,0:T(8,128)(2,1)S(1)} %bitcast.1), channel_id=1, source_target_pairs={{0,64},{4,452},{8,460},{12,72},{16,80},{20,468},{24,476},{28,88},{... | collective-permute-start | bytes 786440 | tf_op jit(solution)/shard_map/ppermute | solution.py:224
  35.1 3.1 %collective-permute-start.4 = (bf16[128,2048]{1,0:T(8,128)(2,1)S(1)}, bf16[128,2048]{1,0:T(8,128)(2,1)S(1)}, u32[]{:S(2)}, u32[]{:S(2)}) collective-permute-start(bf16[128,2048]{1,0:T(8,128)(2,1)S(1)} %constant_dynamic-update-slice_fusion.g0_ref), channel_id=1, source_target_pairs={{0,3},{1,0},{2,1},{3,2},{4,5},{5,6},{6,7},{7,4},{8,11},{9,8},{10,9... | collective-permute-start | bytes 1572872 | tf_op jit(solution)/shard_map/ppermute | solution.py:222
  38.2 0.2 collective-permute-done.a1_ref
  38.3 0.0 collective-permute-done.2.g1_ref
  38.4 5.0 %collective-permute-start.3 = (bf16[256,512]{1,0:T(8,128)(2,1)S(1)}, bf16[256,512]{1,0:T(8,128)(2,1)S(1)}, u32[]{:S(2)}, u32[]{:S(2)}) collective-permute-start(bf16[256,512]{1,0:T(8,128)(2,1)S(1)} %collective-permute-done.a1_ref), channel_id=1, source_target_pairs={{0,64},{4,452},{8,72},{12,460},{16,80},{20,468},{24,88},{28,476},{... | collective-permute-start | bytes 786440 | tf_op jit(solution)/shard_map/ppermute | solution.py:226
  43.4 4.4 %collective-permute-start.7 = (bf16[128,2048]{1,0:T(8,128)(2,1)S(1)}, bf16[128,2048]{1,0:T(8,128)(2,1)S(1)}, u32[]{:S(2)}, u32[]{:S(2)}) collective-permute-start(bf16[128,2048]{1,0:T(8,128)(2,1)S(1)} %collective-permute-done.2.g1_ref), channel_id=1, source_target_pairs={{0,1},{1,2},{2,3},{3,0},{4,7},{5,4},{6,5},{7,6},{8,9},{9,10},{10,1... | collective-permute-start | bytes 1572872 | tf_op jit(solution)/shard_map/ppermute | solution.py:223
  47.8 1.9 %collective-permute-start.6 = (bf16[256,512]{1,0:T(8,128)(2,1)S(1)}, bf16[256,512]{1,0:T(8,128)(2,1)S(1)}, u32[]{:S(2)}, u32[]{:S(2)}) collective-permute-start(bf16[256,512]{1,0:T(8,128)(2,1)S(1)} %collective-permute-done.a1_ref), channel_id=1, source_target_pairs={{0,8},{4,12},{8,0},{12,4},{16,24},{20,28},{24,16},{28,20},{32,40},... | collective-permute-start | bytes 786440 | tf_op jit(solution)/shard_map/ppermute | solution.py:227
  49.7 0.0 collective-permute-done.4.g3_ref
  49.7 0.0 collective-permute-done.3.a2_ref
  49.7 2.1 %collective-permute-start.5 = (bf16[256,512]{1,0:T(8,128)(2,1)S(1)}, bf16[256,512]{1,0:T(8,128)(2,1)S(1)}, u32[]{:S(2)}, u32[]{:S(2)}) collective-permute-start(bf16[256,512]{1,0:T(8,128)(2,1)S(1)} %collective-permute-done.3.a2_ref), channel_id=1, source_target_pairs={{0,64},{4,452},{8,72},{12,460},{16,80},{20,468},{24,88},{28,476},{... | collective-permute-start | bytes 786440 | tf_op jit(solution)/shard_map/ppermute | solution.py:229
  51.8 3.4 %collective-permute-start.8 = (bf16[256,512]{1,0:T(8,128)(2,1)S(1)}, bf16[256,512]{1,0:T(8,128)(2,1)S(1)}, u32[]{:S(2)}, u32[]{:S(2)}) collective-permute-start(bf16[256,512]{1,0:T(8,128)(2,1)S(1)} %collective-permute-done.3.a2_ref), channel_id=1, source_target_pairs={{0,8},{4,12},{8,0},{12,4},{16,24},{20,28},{24,16},{28,20},{32,40},... | collective-permute-start | bytes 786440 | tf_op jit(solution)/shard_map/ppermute | solution.py:230
  55.2 1.1 %collective-permute-done.6.b1_ref = bf16[256,512]{1,0:T(8,128)(2,1)S(1)} collective-permute-done((bf16[256,512]{1,0:T(8,128)(2,1)S(1)}, bf16[256,512]{1,0:T(8,128)(2,1)S(1)}, u32[]{:S(2)}, u32[]{:S(2)}) %collective-permute-start.6) | collective-permute-done | bytes 262176 | tf_op jit(solution)/shard_map/ppermute | solution.py:227
  56.3 0.9 %collective-permute-done.5.a3_ref = bf16[256,512]{1,0:T(8,128)(2,1)S(1)} collective-permute-done((bf16[256,512]{1,0:T(8,128)(2,1)S(1)}, bf16[256,512]{1,0:T(8,128)(2,1)S(1)}, u32[]{:S(2)}, u32[]{:S(2)}) %collective-permute-start.5) | collective-permute-done | bytes 262176 | tf_op jit(solution)/shard_map/ppermute | solution.py:229
  57.1 0.0 collective-permute-done.7.g2_ref
  57.1 3.0 %collective-permute-start.10 = (bf16[256,512]{1,0:T(8,128)(2,1)S(1)}, bf16[256,512]{1,0:T(8,128)(2,1)S(1)}, u32[]{:S(2)}, u32[]{:S(2)}) collective-permute-start(bf16[256,512]{1,0:T(8,128)(2,1)S(1)} %collective-permute-done.5.a3_ref), channel_id=1, source_target_pairs={{0,64},{4,452},{8,72},{12,460},{16,80},{20,468},{24,88},{28,476},{... | collective-permute-start | bytes 786440 | tf_op jit(solution)/shard_map/ppermute | solution.py:232
  60.1 3.4 %collective-permute-start.9 = (bf16[256,512]{1,0:T(8,128)(2,1)S(1)}, bf16[256,512]{1,0:T(8,128)(2,1)S(1)}, u32[]{:S(2)}, u32[]{:S(2)}) collective-permute-start(bf16[256,512]{1,0:T(8,128)(2,1)S(1)} %collective-permute-done.5.a3_ref), channel_id=1, source_target_pairs={{0,8},{4,12},{8,0},{12,4},{16,24},{20,28},{24,16},{28,20},{32,40},... | collective-permute-start | bytes 786440 | tf_op jit(solution)/shard_map/ppermute | solution.py:233
  63.5 0.0 collective-permute-done.8.b2_ref
  63.5 0.8 %shard_map.95.first_ref = f32[512,512]{1,0:T(8,128)S(1)} custom-call(bf16[256,512]{1,0:T(8,128)(2,1)S(1)} %bitcast.2, bf16[256,512]{1,0:T(8,128)(2,1)S(1)} %collective-permute-done.a1_ref, bf16[256,512]{1,0:T(8,128)(2,1)S(1)} %collective-permute-done.6.b1_ref, bf16[256,512]{1,0:T(8,128)(2,1)S(1)} %collective-permute-done.3.a2_ref, ...), custom_call_target="tpu_custom_call" | custom-call | flops 671088640 | bytes 5242880 | tf_op jit(solution)/shard_map/pallas_call | solution.py:242
  64.3 0.0 copy-start.1
  64.4 0.0 copy-start.2
  64.4 0.0 copy-start.3
  64.4 0.0 collective-permute-done.10.a4_ref
  64.4 5.2 %collective-permute-done.9.b3_ref = bf16[256,512]{1,0:T(8,128)(2,1)S(1)} collective-permute-done((bf16[256,512]{1,0:T(8,128)(2,1)S(1)}, bf16[256,512]{1,0:T(8,128)(2,1)S(1)}, u32[]{:S(2)}, u32[]{:S(2)}) %collective-permute-start.9) | collective-permute-done | bytes 262176 | tf_op jit(solution)/shard_map/ppermute | solution.py:233
  69.6 0.0 copy-start.5
  69.6 0.0 copy-start.6
  69.6 0.6 shard_map.96
  70.2 3.1 %collective-permute-start.11 = (f32[256,512]{1,0:T(8,128)S(1)}, f32[256,512]{1,0:T(8,128)S(1)}, u32[]{:S(2)}, u32[]{:S(2)}) collective-permute-start(f32[256,512]{1,0:T(8,128)S(1)} %get-tuple-element.30), channel_id=1, source_target_pairs={{0,4},{4,0},{8,12},{12,8},{16,20},{20,16},{24,28},{28,24},{32,36},... | collective-permute-start | bytes 1572872 | tf_op jit(solution)/shard_map/ppermute | solution.py:248
  73.2 0.0 copy-done.1
  73.2 0.0 copy-done.2
  73.2 0.0 copy-done.3
  73.3 0.0 copy-done.5
  73.3 0.0 copy-done.6
  73.3 2.0 %shard_map.97 = (bf16[256,512]{1,0:T(8,128)(2,1)S(1)}, bf16[256,512]{1,0:T(8,128)(2,1)S(1)}, bf16[256,512]{1,0:T(8,128)(2,1)S(1)}, f32[4,256,256]{2,1,0:T(8,128)...) custom-call(s32[1,512]{1,0:T(1,128)S(1)} %copy-done.5, s32[1,512]{1,0:T(1,128)S(1)} %copy-done.6, ...), custom_call_target="tpu_custom_call" | custom-call | flops 134217728 | bytes 4194304 | tf_op jit(solution)/shard_map/pallas_call | solution.py:234
  75.3 0.0 collective-permute-done.11.other_ref
  75.3 3.2 %shard_map.98 = (bf16[1,512,512]{2,1,0:T(8,128)(2,1)}, bf16[1,512,512]{2,1,0:T(8,128)(2,1)}, bf16[1,512,512]{2,1,0:T(8,128)(2,1)}) custom-call(f32[256,512]{1,0:T(8,128)S(1)} %get-tuple-element.29.mine_ref, f32[256,512]{1,0:T(8,128)S(1)} %collective-permute-done.11.other_ref, bf16[256,512]{1,0:T(8,128)(2,1)S(1)} %get-tuple-element.31.qc_ref, ...), custom_call_target="tpu_custom_call" | custom-call | flops 335544320 | bytes 5242880 | tf_op jit(solution)/shard_map/pallas_call | solution.py:249
  (2 shorter events, 0.0 us)
Async XLA Ops:
  0.6 1.2 %copy-start = (bf16[1,128,4096]{2,1,0:T(8,128)(2,1)S(1)}, bf16[1,128,4096]{2,1,0:T(8,128)(2,1)}, u32[]{:S(2)}) copy-start(bf16[1,128,4096]{2,1,0:T(8,128)(2,1)} %grad_ref.1) | copy-start | bytes 3145732
  1.9 0.7 copy-start.4
  2.5 9.7 %copy-start.7 = (bf16[32,512]{1,0:T(8,128)(2,1)S(1)}, bf16[32,512]{1,0:T(8,128)(2,1)}, u32[]{:S(2)}) copy-start(bf16[32,512]{1,0:T(8,128)(2,1)} %param.11) | copy-start | bytes 98308
  3.4 14.2 %collective-permute-start.1 = (bf16[64,2048]{1,0:T(8,128)(2,1)S(1)}, bf16[64,2048]{1,0:T(8,128)(2,1)S(1)}, u32[]{:S(2)}, u32[]{:S(2)}) collective-permute-start(bf16[64,2048]{1,0:T(8,128)(2,1)S(1)} %get-tuple-element.21), channel_id=1, source_target_pairs={{0,4},{4,0},{8,12},{12,8},{16,20},{20,16},{24,28},{28,24},{32,36},... | collective-permute-start | bytes 786440 | tf_op jit(solution)/shard_map/ppermute | solution.py:217
  12.9 17.0 %all-to-all-start = ((bf16[8,32,512]{2,1,0:T(8,128)(2,1)}), bf16[8,32,512]{2,1,0:T(8,128)(2,1)S(1)}, u32[]{:S(2)}, u32[]{:S(2)}) async-start(bf16[8,32,512]{2,1,0:T(8,128)(2,1)} %broadcast_in_dim.2), calls=%async_computation | async-start | bytes 524288 | tf_op jit(solution)/shard_map/all_to_all | solution.py:220
  17.7 20.7 %collective-permute-start.2 = (bf16[128,2048]{1,0:T(8,128)(2,1)S(1)}, bf16[128,2048]{1,0:T(8,128)(2,1)S(1)}, u32[]{:S(2)}, u32[]{:S(2)}) collective-permute-start(bf16[128,2048]{1,0:T(8,128)(2,1)S(1)} %constant_dynamic-update-slice_fusion.g0_ref), channel_id=1, source_target_pairs={{0,1},{1,2},{2,3},{3,0},{4,7},{5,4},{6,5},{7,6},{8,9},{9,10},{10,1... | collective-permute-start | bytes 1572872 | tf_op jit(solution)/shard_map/ppermute | solution.py:221
  30.0 8.4 %collective-permute-start = (bf16[256,512]{1,0:T(8,128)(2,1)S(1)}, bf16[256,512]{1,0:T(8,128)(2,1)S(1)}, u32[]{:S(2)}, u32[]{:S(2)}) collective-permute-start(bf16[256,512]{1,0:T(8,128)(2,1)S(1)} %bitcast.1), channel_id=1, source_target_pairs={{0,64},{4,452},{8,460},{12,72},{16,80},{20,468},{24,476},{28,88},{... | collective-permute-start | bytes 786440 | tf_op jit(solution)/shard_map/ppermute | solution.py:224
  35.1 14.7 %collective-permute-start.4 = (bf16[128,2048]{1,0:T(8,128)(2,1)S(1)}, bf16[128,2048]{1,0:T(8,128)(2,1)S(1)}, u32[]{:S(2)}, u32[]{:S(2)}) collective-permute-start(bf16[128,2048]{1,0:T(8,128)(2,1)S(1)} %constant_dynamic-update-slice_fusion.g0_ref), channel_id=1, source_target_pairs={{0,3},{1,0},{2,1},{3,2},{4,5},{5,6},{6,7},{7,4},{8,11},{9,8},{10,9... | collective-permute-start | bytes 1572872 | tf_op jit(solution)/shard_map/ppermute | solution.py:222
  38.4 11.4 %collective-permute-start.3 = (bf16[256,512]{1,0:T(8,128)(2,1)S(1)}, bf16[256,512]{1,0:T(8,128)(2,1)S(1)}, u32[]{:S(2)}, u32[]{:S(2)}) collective-permute-start(bf16[256,512]{1,0:T(8,128)(2,1)S(1)} %collective-permute-done.a1_ref), channel_id=1, source_target_pairs={{0,64},{4,452},{8,72},{12,460},{16,80},{20,468},{24,88},{28,476},{... | collective-permute-start | bytes 786440 | tf_op jit(solution)/shard_map/ppermute | solution.py:226
  43.4 13.8 %collective-permute-start.7 = (bf16[128,2048]{1,0:T(8,128)(2,1)S(1)}, bf16[128,2048]{1,0:T(8,128)(2,1)S(1)}, u32[]{:S(2)}, u32[]{:S(2)}) collective-permute-start(bf16[128,2048]{1,0:T(8,128)(2,1)S(1)} %collective-permute-done.2.g1_ref), channel_id=1, source_target_pairs={{0,1},{1,2},{2,3},{3,0},{4,7},{5,4},{6,5},{7,6},{8,9},{9,10},{10,1... | collective-permute-start | bytes 1572872 | tf_op jit(solution)/shard_map/ppermute | solution.py:223
  47.8 8.5 %collective-permute-start.6 = (bf16[256,512]{1,0:T(8,128)(2,1)S(1)}, bf16[256,512]{1,0:T(8,128)(2,1)S(1)}, u32[]{:S(2)}, u32[]{:S(2)}) collective-permute-start(bf16[256,512]{1,0:T(8,128)(2,1)S(1)} %collective-permute-done.a1_ref), channel_id=1, source_target_pairs={{0,8},{4,12},{8,0},{12,4},{16,24},{20,28},{24,16},{28,20},{32,40},... | collective-permute-start | bytes 786440 | tf_op jit(solution)/shard_map/ppermute | solution.py:227
  49.7 7.4 %collective-permute-start.5 = (bf16[256,512]{1,0:T(8,128)(2,1)S(1)}, bf16[256,512]{1,0:T(8,128)(2,1)S(1)}, u32[]{:S(2)}, u32[]{:S(2)}) collective-permute-start(bf16[256,512]{1,0:T(8,128)(2,1)S(1)} %collective-permute-done.3.a2_ref), channel_id=1, source_target_pairs={{0,64},{4,452},{8,72},{12,460},{16,80},{20,468},{24,88},{28,476},{... | collective-permute-start | bytes 786440 | tf_op jit(solution)/shard_map/ppermute | solution.py:229
  51.8 11.7 %collective-permute-start.8 = (bf16[256,512]{1,0:T(8,128)(2,1)S(1)}, bf16[256,512]{1,0:T(8,128)(2,1)S(1)}, u32[]{:S(2)}, u32[]{:S(2)}) collective-permute-start(bf16[256,512]{1,0:T(8,128)(2,1)S(1)} %collective-permute-done.3.a2_ref), channel_id=1, source_target_pairs={{0,8},{4,12},{8,0},{12,4},{16,24},{20,28},{24,16},{28,20},{32,40},... | collective-permute-start | bytes 786440 | tf_op jit(solution)/shard_map/ppermute | solution.py:230
  57.1 7.2 %collective-permute-start.10 = (bf16[256,512]{1,0:T(8,128)(2,1)S(1)}, bf16[256,512]{1,0:T(8,128)(2,1)S(1)}, u32[]{:S(2)}, u32[]{:S(2)}) collective-permute-start(bf16[256,512]{1,0:T(8,128)(2,1)S(1)} %collective-permute-done.5.a3_ref), channel_id=1, source_target_pairs={{0,64},{4,452},{8,72},{12,460},{16,80},{20,468},{24,88},{28,476},{... | collective-permute-start | bytes 786440 | tf_op jit(solution)/shard_map/ppermute | solution.py:232
  60.1 9.5 %collective-permute-start.9 = (bf16[256,512]{1,0:T(8,128)(2,1)S(1)}, bf16[256,512]{1,0:T(8,128)(2,1)S(1)}, u32[]{:S(2)}, u32[]{:S(2)}) collective-permute-start(bf16[256,512]{1,0:T(8,128)(2,1)S(1)} %collective-permute-done.5.a3_ref), channel_id=1, source_target_pairs={{0,8},{4,12},{8,0},{12,4},{16,24},{20,28},{24,16},{28,20},{32,40},... | collective-permute-start | bytes 786440 | tf_op jit(solution)/shard_map/ppermute | solution.py:233
  64.3 8.9 %copy-start.1 = (bf16[1,512,512]{2,1,0:T(8,128)(2,1)S(1)}, bf16[1,512,512]{2,1,0:T(8,128)(2,1)}, u32[]{:S(2)}) copy-start(bf16[1,512,512]{2,1,0:T(8,128)(2,1)} %q_ref.1) | copy-start | bytes 1572868
  64.4 8.9 %copy-start.2 = (bf16[1,512,512]{2,1,0:T(8,128)(2,1)S(1)}, bf16[1,512,512]{2,1,0:T(8,128)(2,1)}, u32[]{:S(2)}) copy-start(bf16[1,512,512]{2,1,0:T(8,128)(2,1)} %k_ref.1) | copy-start | bytes 1572868
  64.4 8.9 %copy-start.3 = (bf16[1,512,512]{2,1,0:T(8,128)(2,1)S(1)}, bf16[1,512,512]{2,1,0:T(8,128)(2,1)}, u32[]{:S(2)}) copy-start(bf16[1,512,512]{2,1,0:T(8,128)(2,1)} %v_ref.1) | copy-start | bytes 1572868
  69.6 3.7 %copy-start.5 = (s32[1,512]{1,0:T(1,128)S(1)}, s32[1,512]{1,0:T(1,128)}, u32[]{:S(2)}) copy-start(s32[1,512]{1,0:T(1,128)} %depths_ref.3) | copy-start | bytes 6148
  69.6 3.7 %copy-start.6 = (s32[1,512]{1,0:T(1,128)S(1)}, s32[1,512]{1,0:T(1,128)}, u32[]{:S(2)}) copy-start(s32[1,512]{1,0:T(1,128)} %documents_ref.1) | copy-start | bytes 6148
  70.2 5.2 %collective-permute-start.11 = (f32[256,512]{1,0:T(8,128)S(1)}, f32[256,512]{1,0:T(8,128)S(1)}, u32[]{:S(2)}, u32[]{:S(2)}) collective-permute-start(f32[256,512]{1,0:T(8,128)S(1)} %get-tuple-element.30), channel_id=1, source_target_pairs={{0,4},{4,0},{8,12},{12,8},{16,20},{20,16},{24,28},{28,24},{32,36},... | collective-permute-start | bytes 1572872 | tf_op jit(solution)/shard_map/ppermute | solution.py:248

commit v3 on v2

--- a/solution.py
+++ b/solution.py
@@ -21,9 +21,11 @@
 COLS = 512
 HEADS = COLS // HD
 VMEM = 48 * 1024 * 1024
+PREP_VMEM = 60 * 1024 * 1024
 NT = (((1,), (1,)), ((), ()))
 TN = (((0,), (0,)), ((), ()))
 bf16, f32 = jnp.bfloat16, jnp.float32
+SENT = bf16
 
 
 def _place(y, z, c):
@@ -65,18 +67,32 @@
     return (slot == rank).astype(bf16)
 
 
-def _cotangent_kernel(depths_ref, grad_ref, keep_ref, send_ref, q_ref, o_ref):
+def _prepare_kernel(
+    depths_any, grad_any, weight_any, copies_ref, keep_ref, send_ref, q_ref, o_ref, depths_ref, grad_ref, weight_ref, sems
+):
+    loads = [
+        pltpu.make_async_copy(depths_any, depths_ref, sems.at[0]),
+        pltpu.make_async_copy(weight_any, weight_ref, sems.at[1]),
+        pltpu.make_async_copy(grad_any, grad_ref, sems.at[2]),
+    ]
+    for load in loads:
+        load.start()
     dp = lax.axis_index("dp")
     x = lax.axis_index("seq")
     core = lax.rem(dp, 2)
     odd = lax.rem(lax.div(dp, 2), 2)
     y = lax.div(dp, 2 * NZ)
     step = 1 - 2 * core
-    sel = _selection(depths_ref[:, pl.ds(pl.multiple_of(x * GROUP, GROUP), GROUP)])
     l = lax.broadcasted_iota(jnp.int32, (256, 256), 0)
     m = lax.broadcasted_iota(jnp.int32, (256, 256), 1)
     other = jnp.bitwise_xor(jnp.bitwise_and(l >> 5, 1), jnp.bitwise_xor(core, odd))
     sort = (m == other * 128 + (l >> 6) * 32 + jnp.bitwise_and(l, 31)).astype(bf16)
+    loads[0].wait()
+    sel = _selection(depths_ref[:, pl.ds(pl.multiple_of(x * GROUP, GROUP), GROUP)])
+    loads[1].wait()
+    for z in range(NZ):
+        copies_ref[z] = weight_ref[...]
+    loads[2].wait()
     rows = _dot(sel, grad_ref[0]).astype(bf16)
     for n in range(D // 256):
         at = slice(n * 128, (n + 1) * 128)
@@ -104,14 +120,14 @@
 
 
 def _softmax_kernel(
-    depths_ref, documents_ref, q_ref, k_ref, v_ref, qc_ref, kc_ref, vc_ref, probs_ref, attended_ref, sel_ref
+    depths_ref, documents_ref, q_ref, k_ref, v_ref, qc_ref, kc_ref, vc_ref, probs_ref, turned_ref, attended_ref, place_ref
 ):
     docs_col, docs_row, valid_col, valid_row = [], [], [], []
     for b in range(NX):
         at = slice(b * GROUP, (b + 1) * GROUP)
         to = slice(b * CAP, (b + 1) * CAP)
         sel = _selection(depths_ref[:, at])
-        sel_ref[to, :] = sel
+        place_ref[at, :] = sel.astype(f32).T.astype(bf16)
         for src, dst in ((q_ref, qc_ref), (k_ref, kc_ref), (v_ref, vc_ref)):
             dst[to, :] = _dot(sel, src[0, at, :]).astype(bf16)
         docs = documents_ref[:, at].astype(f32)
@@ -142,6 +158,7 @@
         total = jnp.where(total > 0.0, total, 1.0)
         probs = raw * (1.0 / total)
         probs_ref[h] = probs
+        turned_ref[h] = probs.T.astype(bf16)
         attended_ref[:, cols] = _dot(probs.astype(bf16), vc_ref[:, cols])
 
 
@@ -160,63 +177,81 @@
     )
 
 
-def _project_last_kernel(
-    first_ref, a3_ref, b3_ref, a4_ref, g0_ref, g1_ref, g2_ref, g3_ref, mine_ref, other_ref
-):
+def _project_last_kernel(own, first_ref, a3_ref, b3_ref, a4_ref, g0_ref, g1_ref, g2_ref, g3_ref, out_ref):
     x = lax.axis_index("seq")
     step = 1 - 2 * lax.rem(lax.axis_index("dp"), 2)
-    total = first_ref[...] + _partial(
-        (g0_ref, g1_ref, g2_ref, g3_ref), (a3_ref, b3_ref, a4_ref), 5 * HALF
-    )
+    part = slice(0, CAP) if own else slice(CAP, 2 * CAP)
+    gs = [g.at[part] for g in (g0_ref, g1_ref, g2_ref, g3_ref)]
+    total = _partial(gs, (a3_ref, b3_ref, a4_ref), 5 * HALF)
     for n, shift in enumerate((0, -step, 2, step)):
         at = pl.ds(pl.multiple_of(lax.rem(x + shift + NX, NX) * CAP, CAP), CAP)
-        mine_ref[at, :] = total[2 * n * CAP : (2 * n + 1) * CAP]
-        other_ref[at, :] = total[(2 * n + 1) * CAP : (2 * n + 2) * CAP]
+        frm = slice(2 * n * CAP + part.start, 2 * n * CAP + part.stop)
+        out_ref[at, :] = (total[n * CAP : (n + 1) * CAP] + first_ref[frm, :]).astype(out_ref.dtype)
 
 
 def _gradients_kernel(
-    mine_ref, other_ref, qc_ref, kc_ref, vc_ref, probs_ref, attended_ref, sel_ref, dq_ref, dk_ref, dv_ref
+    mine_ref, other_ref, qc_ref, kc_ref, vc_ref, probs_ref, turned_ref, attended_ref, place_ref,
+    dq_any, dk_any, dv_any, og_ref, rows_ref, dq_ref, dk_ref, dv_ref, sems,
 ):
     scale = HD ** (-0.5)
-    for h in range(HEADS):
-        cols = slice(h * HD, (h + 1) * HD)
-        out_grad = (mine_ref[:, cols] + other_ref[:, cols]).astype(bf16)
-        q, k, v = qc_ref[:, cols], kc_ref[:, cols], vc_ref[:, cols]
-        probs = probs_ref[h]
-        delta = jnp.sum(out_grad.astype(f32) * attended_ref[:, cols], axis=1, keepdims=True)
-        dscore = (probs * (_dot(out_grad, v, NT) - delta)).astype(bf16)
-        dv = _dot(probs.astype(bf16), out_grad, TN).astype(bf16)
-        dq = (_dot(dscore, k) * scale).astype(bf16)
-        dk = (_dot(dscore, q, TN) * scale).astype(bf16)
+    og_ref[...] = (mine_ref[...] + other_ref[...].astype(f32)).astype(bf16)
+    heads = [slice(h * HD, (h + 1) * HD) for h in range(HEADS)]
+
+    def finish(n, full_ref, out_any):
         for b in range(NX):
             at = slice(b * GROUP, (b + 1) * GROUP)
-            frm = slice(b * CAP, (b + 1) * CAP)
-            sel = sel_ref[frm, :]
-            for src, dst in ((dq, dq_ref), (dk, dk_ref), (dv, dv_ref)):
-                dst[0, at, cols] = _dot(sel, src[frm, :], TN).astype(bf16)
-
-
-def _call(kernel, outs, flops, nbytes, exps=0, scratch=()):
+            full_ref[0, at, :] = _dot(place_ref[at, :], rows_ref[n, b * CAP : (b + 1) * CAP, :]).astype(bf16)
+        copy = pltpu.make_async_copy(full_ref, out_any, sems.at[n])
+        copy.start()
+        return copy
+
+    for h, cols in enumerate(heads):
+        rows_ref[2, :, cols] = _dot(turned_ref[h], og_ref[:, cols]).astype(bf16)
+    copies = [finish(2, dv_ref, dv_any)]
+    dscores = []
+    for h, cols in enumerate(heads):
+        out_grad = og_ref[:, cols]
+        delta = jnp.sum(out_grad.astype(f32) * attended_ref[:, cols], axis=1, keepdims=True)
+        dscore = (probs_ref[h] * (_dot(out_grad, vc_ref[:, cols], NT) - delta)).astype(bf16)
+        rows_ref[0, :, cols] = (_dot(dscore, kc_ref[:, cols]) * scale).astype(bf16)
+        dscores.append(dscore)
+    copies.append(finish(0, dq_ref, dq_any))
+    for h, cols in enumerate(heads):
+        rows_ref[1, :, cols] = (_dot(dscores[h], qc_ref[:, cols], TN) * scale).astype(bf16)
+    copies.append(finish(1, dk_ref, dk_any))
+    for copy in copies:
+        copy.wait()
+
+
+def _call(kernel, outs, flops, nbytes, exps=0, scratch=(), vmem=VMEM, **specs):
     return pl.pallas_call(
         kernel,
         out_shape=tuple(jax.ShapeDtypeStruct(s, t) for s, t in outs),
         scratch_shapes=scratch,
-        compiler_params=pltpu.CompilerParams(vmem_limit_bytes=VMEM),
+        **specs,
+        compiler_params=pltpu.CompilerParams(vmem_limit_bytes=vmem),
         cost_estimate=pl.CostEstimate(flops=flops, bytes_accessed=nbytes, transcendentals=exps),
     )
 
 
 def on_device(queries, key_states, value_states, grad_out, out_weight, depths, documents):
-    keep, send = _call(
-        _cotangent_kernel,
-        [((CAP, KC), bf16)] * 2,
+    copies, keep, send = _call(
+        _prepare_kernel,
+        [((NZ, D // (NY * NZ * 2), COLS), bf16)] + [((CAP, KC), bf16)] * 2,
         2 * CAP * D * (GROUP + 256),
         2 << 20,
-        scratch=[pltpu.VMEM((CAP, KC), bf16)] * 2,
-    )(depths, grad_out)
+        scratch=[pltpu.VMEM((CAP, KC), bf16)] * 2
+        + [
+            pltpu.VMEM((1, SEQ), jnp.int32),
+            pltpu.VMEM((1, GROUP, D), bf16),
+            pltpu.VMEM((D // (NY * NZ * 2), COLS), bf16),
+            pltpu.SemaphoreType.DMA((3,)),
+        ],
+        vmem=PREP_VMEM,
+        in_specs=[pl.BlockSpec(memory_space=pl.ANY)] * 3,
+    )(depths, grad_out, out_weight)
     got = lax.ppermute(send, "dp", SWAP)
     g0 = jnp.concatenate([keep, got], axis=0)
-    copies = jnp.broadcast_to(out_weight[None], (NZ,) + out_weight.shape)
     own = lax.all_to_all(copies, "dp", 0, 0, axis_index_groups=Z_GROUPS).reshape(HALF, COLS)
     g1 = lax.ppermute(g0, ("dp", "seq"), X_ALONG)
     g3 = lax.ppermute(g0, ("dp", "seq"), X_AGAINST)
@@ -231,10 +266,10 @@
     a3, b1, g2 = lax.optimization_barrier((a3, b1, g2))
     a4 = lax.ppermute(a3, "dp", Y_ALONG)
     b3 = lax.ppermute(a3, "dp", Z_SWAP)
-    qc, kc, vc, probs, attended, sel = _call(
+    qc, kc, vc, probs, turned, attended, place = _call(
         _softmax_kernel,
         [((ROWS, COLS), bf16)] * 3
-        + [((HEADS, ROWS, ROWS), f32), ((ROWS, COLS), f32), ((ROWS, GROUP), bf16)],
+        + [((HEADS, ROWS, ROWS), f32), ((HEADS, ROWS, ROWS), bf16), ((ROWS, COLS), f32), ((SEQ, CAP), bf16)],
         4 * HEADS * ROWS * ROWS * HD,
         4 << 20,
         HEADS * ROWS * ROWS,
@@ -242,13 +277,25 @@
     first = _call(
         _project_first_kernel, [((2 * ROWS, COLS), f32)], 20 * ROWS * HALF * COLS, 5 << 20
     )(own, a1, b1, a2, b2, g0, g1, g2, g3)[0]
-    mine, other = _call(
-        _project_last_kernel, [((ROWS, COLS), f32)] * 2, 12 * ROWS * HALF * COLS, 5 << 20
-    )(first, a3, b3, a4, g0, g1, g2, g3)
-    theirs = lax.ppermute(other, "dp", SWAP)
+    first, probs = lax.optimization_barrier((first, probs))
+    last = (first, a3, b3, a4, g0, g1, g2, g3)
+    other = _call(
+        functools.partial(_project_last_kernel, False), [((ROWS, COLS), SENT)], 6 * ROWS * HALF * COLS, 3 << 20
+    )(*last)[0]
+    swapped = lax.ppermute(other, "dp", SWAP)
+    mine = _call(
+        functools.partial(_project_last_kernel, True), [((ROWS, COLS), f32)], 6 * ROWS * HALF * COLS, 3 << 20
+    )(*last)[0]
     return _call(
-        _gradients_kernel, [((1, SEQ, COLS), bf16)] * 3, 10 * HEADS * ROWS * ROWS * HD, 5 << 20
-    )(mine, theirs, qc, kc, vc, probs, attended, sel)
+        _gradients_kernel,
+        [((1, SEQ, COLS), bf16)] * 3,
+        10 * HEADS * ROWS * ROWS * HD,
+        5 << 20,
+        scratch=[pltpu.VMEM((ROWS, COLS), bf16), pltpu.VMEM((3, ROWS, COLS), bf16)]
+        + [pltpu.VMEM((1, SEQ, COLS), bf16)] * 3
+        + [pltpu.SemaphoreType.DMA((3,))],
+        out_specs=tuple([pl.BlockSpec(memory_space=pl.ANY)] * 3),
+    )(mine, swapped, qc, kc, vc, probs, turned, attended, place)
 
 
 def solution(mesh):

time: 79.4 us -> 76.9 us (0.969)
  waiting for transfers between devices: 15.3 us -> 12.9 us
  local copies, waits for them, and re-layouts: 2.69 us -> 1.1 us
  Pallas kernels: 7.53 us -> 8.92 us
    pallas_call x2 -> x3, Pallas kernels: 1.43 us -> 3.53 us  [the longest x1 2.79 us: on_device(): _call(_prepare_kernel, [((NZ, D // (NY * NZ * 2), COLS), bf16)] + [((CAP,...]
    ppermute x1, waiting for transfers between devices: 5.2 us -> 3.13 us  [on_device(): b3 = lax.ppermute(a3, 'dp', Z_SWAP)]
    all_to_all x1, waiting for transfers between devices: 7.91 us -> 6.86 us  [on_device(): lax.all_to_all(copies, 'dp', 0, 0, axis_index_groups=Z_GROUPS)]
    unnamed x17 -> x11, local copies, waits for them, and re-layouts: 1.95 us -> 1.08 us
  transfers between devices with their start and end apart: 13 -> 13, of which waited for: 5 -> 6; matrix products, arithmetic and copies ran while one was open for 1% -> 1% of each run, Pallas kernels for 4% -> 4%
where the time goes in v3:
time: 76.9 us; the launch traced here: 76.1 us
  starting transfers between devices  52.3 us (68%)
  waiting for transfers between devices  12.9 us (17%)
  Pallas kernels  8.92 us (12%)
  local copies, waits for them, and re-layouts  1.1 us (1%)
  between operations  0.88 us (1%)
    ppermute x1, starting transfers between devices, on_device(): got = lax.ppermute(send, 'dp', SWAP)  8.79 us
    all_to_all x1, waiting for transfers between devices, on_device(): lax.all_to_all(copies, 'dp', 0, 0, axis_index_groups=Z_GROUPS)  6.86 us
    ppermute x1, starting transfers between devices, on_device(): a1 = lax.ppermute(own, 'dp', Y_FIRST)  5.08 us
    ppermute x1, starting transfers between devices, on_device(): a2 = lax.ppermute(a1, 'dp', Y_ALONG)  5.01 us
    all_to_all x1, starting transfers between devices, on_device(): lax.all_to_all(copies, 'dp', 0, 0, axis_index_groups=Z_GROUPS)  4.81 us
    ppermute x1, starting transfers between devices, on_device(): g2 = lax.ppermute(g1, ('dp', 'seq'), X_ALONG)  4.39 us
    ppermute x1, starting transfers between devices, on_device(): g1 = lax.ppermute(g0, ('dp', 'seq'), X_ALONG)  4.38 us
    ppermute x1, starting transfers between devices, on_device(): b2 = lax.ppermute(a2, 'dp', Z_SWAP)  3.36 us
  transfers between devices with their start and end apart: 13, of which 6 were waited for; matrix products, arithmetic and copies ran while one was open for 1% of the time, Pallas kernels for 4%

profile of v3, /device:TPU:1, one launch (start us, length us, event | category | flops | bytes accessed | tf_op | source)
XLA Modules:
  0.0 76.1 jit_solution(1272326696702397033)
XLA Ops:
  0.6 0.0 copy-start.4
  0.6 2.8 %shard_map.94 = (bf16[8,32,512]{2,1,0:T(8,128)(2,1)}, bf16[64,2048]{1,0:T(8,128)(2,1)}, bf16[64,2048]{1,0:T(8,128)(2,1)}) custom-call(s32[1,512]{1,0:T(1,128)} %depths_ref.1, bf16[1,128,4096]{2,1,0:T(8,128)(2,1)} %grad_any.1, bf16[32,512]{1,0:T(8,128)(2,1)} %weight_any.1), custom_call_target="tpu_custom_call" | custom-call | flops 201326592 | bytes 2097152 | tf_op jit(solution)/shard_map/pallas_call | solution.py:238
  3.4 8.8 %collective-permute-start.1 = (bf16[64,2048]{1,0:T(8,128)(2,1)}, bf16[64,2048]{1,0:T(8,128)(2,1)S(1)}, u32[]{:S(2)}, u32[]{:S(2)}) collective-permute-start(bf16[64,2048]{1,0:T(8,128)(2,1)} %get-tuple-element.24), channel_id=1, source_target_pairs={{0,4},{4,0},{8,12},{12,8},{16,20},{20,16},{24,28},{28,24},{32,36},... | collective-permute-start | bytes 786440 | tf_op jit(solution)/shard_map/ppermute | solution.py:253
  12.2 0.0 copy-start.2
  12.2 0.0 copy-start.3
  12.3 4.8 %all-to-all-start = ((bf16[8,32,512]{2,1,0:T(8,128)(2,1)}), bf16[8,32,512]{2,1,0:T(8,128)(2,1)S(1)}, u32[]{:S(2)}, u32[]{:S(2)}) async-start(bf16[8,32,512]{2,1,0:T(8,128)(2,1)} %get-tuple-element.22), calls=%async_computation | async-start | bytes 524288 | tf_op jit(solution)/shard_map/all_to_all | solution.py:255
  17.1 0.0 copy-start
  17.1 0.0 copy-start.1
  17.1 1.1 %constant_dynamic-update-slice_fusion.1 = bf16[128,2048]{1,0:T(8,128)(2,1)S(1)} fusion(bf16[64,2048]{1,0:T(8,128)(2,1)} %get-tuple-element.23), kind=kLoop, calls=%fused_computation.1 | loop fusion | bytes 524288
  18.1 0.0 collective-permute-done.1
  18.2 4.4 %collective-permute-start.2 = (bf16[128,2048]{1,0:T(8,128)(2,1)S(1)}, bf16[128,2048]{1,0:T(8,128)(2,1)S(1)}, u32[]{:S(2)}, u32[]{:S(2)}) collective-permute-start(bf16[128,2048]{1,0:T(8,128)(2,1)S(1)} %constant_dynamic-update-slice_fusion.g0_ref), channel_id=1, source_target_pairs={{0,1},{1,2},{2,3},{3,0},{4,7},{5,4},{6,5},{7,6},{8,9},{9,10},{10,1... | collective-permute-start | bytes 1572872 | tf_op jit(solution)/shard_map/ppermute | solution.py:256
  22.6 6.9 %all-to-all-done = bf16[8,32,512]{2,1,0:T(8,128)(2,1)S(1)} async-done(((bf16[8,32,512]{2,1,0:T(8,128)(2,1)}), bf16[8,32,512]{2,1,0:T(8,128)(2,1)S(1)}, u32[]{:S(2)}, u32[]{:S(2)}) %all-to-all-start) | async-done | bytes 262176 | tf_op jit(solution)/shard_map/all_to_all | solution.py:255
  29.4 5.1 %collective-permute-start = (bf16[256,512]{1,0:T(8,128)(2,1)S(1)}, bf16[256,512]{1,0:T(8,128)(2,1)S(1)}, u32[]{:S(2)}, u32[]{:S(2)}) collective-permute-start(bf16[256,512]{1,0:T(8,128)(2,1)S(1)} %bitcast.1), channel_id=1, source_target_pairs={{0,64},{4,452},{8,460},{12,72},{16,80},{20,468},{24,476},{28,88},{... | collective-permute-start | bytes 786440 | tf_op jit(solution)/shard_map/ppermute | solution.py:259
  34.5 3.1 %collective-permute-start.4 = (bf16[128,2048]{1,0:T(8,128)(2,1)S(1)}, bf16[128,2048]{1,0:T(8,128)(2,1)S(1)}, u32[]{:S(2)}, u32[]{:S(2)}) collective-permute-start(bf16[128,2048]{1,0:T(8,128)(2,1)S(1)} %constant_dynamic-update-slice_fusion.g0_ref), channel_id=1, source_target_pairs={{0,3},{1,0},{2,1},{3,2},{4,5},{5,6},{6,7},{7,4},{8,11},{9,8},{10,9... | collective-permute-start | bytes 1572872 | tf_op jit(solution)/shard_map/ppermute | solution.py:257
  37.7 0.2 collective-permute-done.a1_ref
  37.8 0.0 collective-permute-done.2.g1_ref
  37.8 5.0 %collective-permute-start.3 = (bf16[256,512]{1,0:T(8,128)(2,1)S(1)}, bf16[256,512]{1,0:T(8,128)(2,1)S(1)}, u32[]{:S(2)}, u32[]{:S(2)}) collective-permute-start(bf16[256,512]{1,0:T(8,128)(2,1)S(1)} %collective-permute-done.a1_ref), channel_id=1, source_target_pairs={{0,64},{4,452},{8,72},{12,460},{16,80},{20,468},{24,88},{28,476},{... | collective-permute-start | bytes 786440 | tf_op jit(solution)/shard_map/ppermute | solution.py:261
  42.8 4.4 %collective-permute-start.7 = (bf16[128,2048]{1,0:T(8,128)(2,1)S(1)}, bf16[128,2048]{1,0:T(8,128)(2,1)S(1)}, u32[]{:S(2)}, u32[]{:S(2)}) collective-permute-start(bf16[128,2048]{1,0:T(8,128)(2,1)S(1)} %collective-permute-done.2.g1_ref), channel_id=1, source_target_pairs={{0,1},{1,2},{2,3},{3,0},{4,7},{5,4},{6,5},{7,6},{8,9},{9,10},{10,1... | collective-permute-start | bytes 1572872 | tf_op jit(solution)/shard_map/ppermute | solution.py:258
  47.2 1.9 %collective-permute-start.6 = (bf16[256,512]{1,0:T(8,128)(2,1)S(1)}, bf16[256,512]{1,0:T(8,128)(2,1)S(1)}, u32[]{:S(2)}, u32[]{:S(2)}) collective-permute-start(bf16[256,512]{1,0:T(8,128)(2,1)S(1)} %collective-permute-done.a1_ref), channel_id=1, source_target_pairs={{0,8},{4,12},{8,0},{12,4},{16,24},{20,28},{24,16},{28,20},{32,40},... | collective-permute-start | bytes 786440 | tf_op jit(solution)/shard_map/ppermute | solution.py:262
  49.2 0.0 collective-permute-done.4.g3_ref
  49.2 0.0 collective-permute-done.3.a2_ref
  49.2 2.1 %collective-permute-start.5 = (bf16[256,512]{1,0:T(8,128)(2,1)S(1)}, bf16[256,512]{1,0:T(8,128)(2,1)S(1)}, u32[]{:S(2)}, u32[]{:S(2)}) collective-permute-start(bf16[256,512]{1,0:T(8,128)(2,1)S(1)} %collective-permute-done.3.a2_ref), channel_id=1, source_target_pairs={{0,64},{4,452},{8,72},{12,460},{16,80},{20,468},{24,88},{28,476},{... | collective-permute-start | bytes 786440 | tf_op jit(solution)/shard_map/ppermute | solution.py:264
  51.3 3.4 %collective-permute-start.8 = (bf16[256,512]{1,0:T(8,128)(2,1)S(1)}, bf16[256,512]{1,0:T(8,128)(2,1)S(1)}, u32[]{:S(2)}, u32[]{:S(2)}) collective-permute-start(bf16[256,512]{1,0:T(8,128)(2,1)S(1)} %collective-permute-done.3.a2_ref), channel_id=1, source_target_pairs={{0,8},{4,12},{8,0},{12,4},{16,24},{20,28},{24,16},{28,20},{32,40},... | collective-permute-start | bytes 786440 | tf_op jit(solution)/shard_map/ppermute | solution.py:265
  54.6 1.1 %collective-permute-done.6.b1_ref = bf16[256,512]{1,0:T(8,128)(2,1)S(1)} collective-permute-done((bf16[256,512]{1,0:T(8,128)(2,1)S(1)}, bf16[256,512]{1,0:T(8,128)(2,1)S(1)}, u32[]{:S(2)}, u32[]{:S(2)}) %collective-permute-start.6) | collective-permute-done | bytes 262176 | tf_op jit(solution)/shard_map/ppermute | solution.py:262
  55.7 0.9 %collective-permute-done.5.a3_ref = bf16[256,512]{1,0:T(8,128)(2,1)S(1)} collective-permute-done((bf16[256,512]{1,0:T(8,128)(2,1)S(1)}, bf16[256,512]{1,0:T(8,128)(2,1)S(1)}, u32[]{:S(2)}, u32[]{:S(2)}) %collective-permute-start.5) | collective-permute-done | bytes 262176 | tf_op jit(solution)/shard_map/ppermute | solution.py:264
  56.6 0.0 collective-permute-done.7.g2_ref
  56.6 3.0 %collective-permute-start.10 = (bf16[256,512]{1,0:T(8,128)(2,1)S(1)}, bf16[256,512]{1,0:T(8,128)(2,1)S(1)}, u32[]{:S(2)}, u32[]{:S(2)}) collective-permute-start(bf16[256,512]{1,0:T(8,128)(2,1)S(1)} %collective-permute-done.5.a3_ref), channel_id=1, source_target_pairs={{0,64},{4,452},{8,72},{12,460},{16,80},{20,468},{24,88},{28,476},{... | collective-permute-start | bytes 786440 | tf_op jit(solution)/shard_map/ppermute | solution.py:267
  59.6 3.4 %collective-permute-start.9 = (bf16[256,512]{1,0:T(8,128)(2,1)S(1)}, bf16[256,512]{1,0:T(8,128)(2,1)S(1)}, u32[]{:S(2)}, u32[]{:S(2)}) collective-permute-start(bf16[256,512]{1,0:T(8,128)(2,1)S(1)} %collective-permute-done.5.a3_ref), channel_id=1, source_target_pairs={{0,8},{4,12},{8,0},{12,4},{16,24},{20,28},{24,16},{28,20},{32,40},... | collective-permute-start | bytes 786440 | tf_op jit(solution)/shard_map/ppermute | solution.py:268
  62.9 0.0 copy-done.4
  63.0 0.0 copy-done.2
  63.0 0.0 copy-done.3
  63.0 0.0 copy-done
  63.0 0.0 copy-done.1
  63.0 2.0 %shard_map.96 = (bf16[256,512]{1,0:T(8,128)(2,1)S(1)}, bf16[256,512]{1,0:T(8,128)(2,1)S(1)}, bf16[256,512]{1,0:T(8,128)(2,1)S(1)}, f32[4,256,256]{2,1,0:T(8,128)...) custom-call(s32[1,512]{1,0:T(1,128)S(1)} %copy-done.3, ...), custom_call_target="tpu_custom_call" | custom-call | flops 134217728 | bytes 4194304 | tf_op jit(solution)/shard_map/pallas_call | solution.py:269
  65.0 0.0 collective-permute-done.8.b2_ref
  65.0 0.8 %shard_map.95.first_ref = f32[512,512]{1,0:T(8,128)S(1)} custom-call(bf16[256,512]{1,0:T(8,128)(2,1)S(1)} %bitcast.2, bf16[256,512]{1,0:T(8,128)(2,1)S(1)} %collective-permute-done.a1_ref, bf16[256,512]{1,0:T(8,128)(2,1)S(1)} %collective-permute-done.6.b1_ref, bf16[256,512]{1,0:T(8,128)(2,1)S(1)} %collective-permute-done.3.a2_ref, ...), custom_call_target="tpu_custom_call" | custom-call | flops 671088640 | bytes 5242880 | tf_op jit(solution)/shard_map/pallas_call | solution.py:277
  65.9 0.0 collective-permute-done.10.a4_ref
  65.9 3.1 %collective-permute-done.9.b3_ref = bf16[256,512]{1,0:T(8,128)(2,1)S(1)} collective-permute-done((bf16[256,512]{1,0:T(8,128)(2,1)S(1)}, bf16[256,512]{1,0:T(8,128)(2,1)S(1)}, u32[]{:S(2)}, u32[]{:S(2)}) %collective-permute-start.9) | collective-permute-done | bytes 262176 | tf_op jit(solution)/shard_map/ppermute | solution.py:268
  69.0 0.4 shard_map.98
  69.4 3.1 %collective-permute-start.11 = (bf16[256,512]{1,0:T(8,128)(2,1)S(1)}, bf16[256,512]{1,0:T(8,128)(2,1)S(1)}, u32[]{:S(2)}, u32[]{:S(2)}) collective-permute-start(bf16[256,512]{1,0:T(8,128)(2,1)S(1)} %shard_map.98), channel_id=1, source_target_pairs={{0,4},{4,0},{8,12},{12,8},{16,20},{20,16},{24,28},{28,24},{32,36},... | collective-permute-start | bytes 786440 | tf_op jit(solution)/shard_map/ppermute | solution.py:285
  72.5 0.4 shard_map.97.mine_ref
  72.9 0.8 collective-permute-done.11.other_ref
  73.6 2.5 %shard_map.99 = (bf16[1,512,512]{2,1,0:T(8,128)(2,1)}, bf16[1,512,512]{2,1,0:T(8,128)(2,1)}, bf16[1,512,512]{2,1,0:T(8,128)(2,1)}) custom-call(f32[256,512]{1,0:T(8,128)S(1)} %shard_map.97.mine_ref, bf16[256,512]{1,0:T(8,128)(2,1)S(1)} %collective-permute-done.11.other_ref, bf16[256,512]{1,0:T(8,128)(2,1)S(1)} %get-tuple-element.34.qc_ref, ...), custom_call_target="tpu_custom_call" | custom-call | flops 335544320 | bytes 5242880 | tf_op jit(solution)/shard_map/pallas_call | solution.py:289
  (1 shorter events, 0.0 us)
Async XLA Ops:
  0.6 62.3 %copy-start.4 = (s32[1,512]{1,0:T(1,128)S(1)}, s32[1,512]{1,0:T(1,128)}, u32[]{:S(2)}) copy-start(s32[1,512]{1,0:T(1,128)} %documents_ref.1) | copy-start | bytes 6148
  3.4 14.7 %collective-permute-start.1 = (bf16[64,2048]{1,0:T(8,128)(2,1)}, bf16[64,2048]{1,0:T(8,128)(2,1)S(1)}, u32[]{:S(2)}, u32[]{:S(2)}) collective-permute-start(bf16[64,2048]{1,0:T(8,128)(2,1)} %get-tuple-element.24), channel_id=1, source_target_pairs={{0,4},{4,0},{8,12},{12,8},{16,20},{20,16},{24,28},{28,24},{32,36},... | collective-permute-start | bytes 786440 | tf_op jit(solution)/shard_map/ppermute | solution.py:253
  12.2 50.7 %copy-start.2 = (bf16[1,512,512]{2,1,0:T(8,128)(2,1)S(1)}, bf16[1,512,512]{2,1,0:T(8,128)(2,1)}, u32[]{:S(2)}) copy-start(bf16[1,512,512]{2,1,0:T(8,128)(2,1)} %v_ref.1) | copy-start | bytes 1572868
  12.2 50.7 %copy-start.3 = (s32[1,512]{1,0:T(1,128)S(1)}, s32[1,512]{1,0:T(1,128)}, u32[]{:S(2)}) copy-start(s32[1,512]{1,0:T(1,128)} %depths_ref.1) | copy-start | bytes 6148
  12.3 17.2 %all-to-all-start = ((bf16[8,32,512]{2,1,0:T(8,128)(2,1)}), bf16[8,32,512]{2,1,0:T(8,128)(2,1)S(1)}, u32[]{:S(2)}, u32[]{:S(2)}) async-start(bf16[8,32,512]{2,1,0:T(8,128)(2,1)} %get-tuple-element.22), calls=%async_computation | async-start | bytes 524288 | tf_op jit(solution)/shard_map/all_to_all | solution.py:255
  17.1 45.9 %copy-start = (bf16[1,512,512]{2,1,0:T(8,128)(2,1)S(1)}, bf16[1,512,512]{2,1,0:T(8,128)(2,1)}, u32[]{:S(2)}) copy-start(bf16[1,512,512]{2,1,0:T(8,128)(2,1)} %q_ref.1) | copy-start | bytes 1572868
  17.1 45.9 %copy-start.1 = (bf16[1,512,512]{2,1,0:T(8,128)(2,1)S(1)}, bf16[1,512,512]{2,1,0:T(8,128)(2,1)}, u32[]{:S(2)}) copy-start(bf16[1,512,512]{2,1,0:T(8,128)(2,1)} %k_ref.1) | copy-start | bytes 1572868
  18.2 19.6 %collective-permute-start.2 = (bf16[128,2048]{1,0:T(8,128)(2,1)S(1)}, bf16[128,2048]{1,0:T(8,128)(2,1)S(1)}, u32[]{:S(2)}, u32[]{:S(2)}) collective-permute-start(bf16[128,2048]{1,0:T(8,128)(2,1)S(1)} %constant_dynamic-update-slice_fusion.g0_ref), channel_id=1, source_target_pairs={{0,1},{1,2},{2,3},{3,0},{4,7},{5,4},{6,5},{7,6},{8,9},{9,10},{10,1... | collective-permute-start | bytes 1572872 | tf_op jit(solution)/shard_map/ppermute | solution.py:256
  29.4 8.4 %collective-permute-start = (bf16[256,512]{1,0:T(8,128)(2,1)S(1)}, bf16[256,512]{1,0:T(8,128)(2,1)S(1)}, u32[]{:S(2)}, u32[]{:S(2)}) collective-permute-start(bf16[256,512]{1,0:T(8,128)(2,1)S(1)} %bitcast.1), channel_id=1, source_target_pairs={{0,64},{4,452},{8,460},{12,72},{16,80},{20,468},{24,476},{28,88},{... | collective-permute-start | bytes 786440 | tf_op jit(solution)/shard_map/ppermute | solution.py:259
  34.5 14.6 %collective-permute-start.4 = (bf16[128,2048]{1,0:T(8,128)(2,1)S(1)}, bf16[128,2048]{1,0:T(8,128)(2,1)S(1)}, u32[]{:S(2)}, u32[]{:S(2)}) collective-permute-start(bf16[128,2048]{1,0:T(8,128)(2,1)S(1)} %constant_dynamic-update-slice_fusion.g0_ref), channel_id=1, source_target_pairs={{0,3},{1,0},{2,1},{3,2},{4,5},{5,6},{6,7},{7,4},{8,11},{9,8},{10,9... | collective-permute-start | bytes 1572872 | tf_op jit(solution)/shard_map/ppermute | solution.py:257
  37.8 11.4 %collective-permute-start.3 = (bf16[256,512]{1,0:T(8,128)(2,1)S(1)}, bf16[256,512]{1,0:T(8,128)(2,1)S(1)}, u32[]{:S(2)}, u32[]{:S(2)}) collective-permute-start(bf16[256,512]{1,0:T(8,128)(2,1)S(1)} %collective-permute-done.a1_ref), channel_id=1, source_target_pairs={{0,64},{4,452},{8,72},{12,460},{16,80},{20,468},{24,88},{28,476},{... | collective-permute-start | bytes 786440 | tf_op jit(solution)/shard_map/ppermute | solution.py:261
  42.8 13.8 %collective-permute-start.7 = (bf16[128,2048]{1,0:T(8,128)(2,1)S(1)}, bf16[128,2048]{1,0:T(8,128)(2,1)S(1)}, u32[]{:S(2)}, u32[]{:S(2)}) collective-permute-start(bf16[128,2048]{1,0:T(8,128)(2,1)S(1)} %collective-permute-done.2.g1_ref), channel_id=1, source_target_pairs={{0,1},{1,2},{2,3},{3,0},{4,7},{5,4},{6,5},{7,6},{8,9},{9,10},{10,1... | collective-permute-start | bytes 1572872 | tf_op jit(solution)/shard_map/ppermute | solution.py:258
  47.2 8.5 %collective-permute-start.6 = (bf16[256,512]{1,0:T(8,128)(2,1)S(1)}, bf16[256,512]{1,0:T(8,128)(2,1)S(1)}, u32[]{:S(2)}, u32[]{:S(2)}) collective-permute-start(bf16[256,512]{1,0:T(8,128)(2,1)S(1)} %collective-permute-done.a1_ref), channel_id=1, source_target_pairs={{0,8},{4,12},{8,0},{12,4},{16,24},{20,28},{24,16},{28,20},{32,40},... | collective-permute-start | bytes 786440 | tf_op jit(solution)/shard_map/ppermute | solution.py:262
  49.2 7.4 %collective-permute-start.5 = (bf16[256,512]{1,0:T(8,128)(2,1)S(1)}, bf16[256,512]{1,0:T(8,128)(2,1)S(1)}, u32[]{:S(2)}, u32[]{:S(2)}) collective-permute-start(bf16[256,512]{1,0:T(8,128)(2,1)S(1)} %collective-permute-done.3.a2_ref), channel_id=1, source_target_pairs={{0,64},{4,452},{8,72},{12,460},{16,80},{20,468},{24,88},{28,476},{... | collective-permute-start | bytes 786440 | tf_op jit(solution)/shard_map/ppermute | solution.py:264
  51.3 13.8 %collective-permute-start.8 = (bf16[256,512]{1,0:T(8,128)(2,1)S(1)}, bf16[256,512]{1,0:T(8,128)(2,1)S(1)}, u32[]{:S(2)}, u32[]{:S(2)}) collective-permute-start(bf16[256,512]{1,0:T(8,128)(2,1)S(1)} %collective-permute-done.3.a2_ref), channel_id=1, source_target_pairs={{0,8},{4,12},{8,0},{12,4},{16,24},{20,28},{24,16},{28,20},{32,40},... | collective-permute-start | bytes 786440 | tf_op jit(solution)/shard_map/ppermute | solution.py:265
  56.6 9.3 %collective-permute-start.10 = (bf16[256,512]{1,0:T(8,128)(2,1)S(1)}, bf16[256,512]{1,0:T(8,128)(2,1)S(1)}, u32[]{:S(2)}, u32[]{:S(2)}) collective-permute-start(bf16[256,512]{1,0:T(8,128)(2,1)S(1)} %collective-permute-done.5.a3_ref), channel_id=1, source_target_pairs={{0,64},{4,452},{8,72},{12,460},{16,80},{20,468},{24,88},{28,476},{... | collective-permute-start | bytes 786440 | tf_op jit(solution)/shard_map/ppermute | solution.py:267
  59.6 9.5 %collective-permute-start.9 = (bf16[256,512]{1,0:T(8,128)(2,1)S(1)}, bf16[256,512]{1,0:T(8,128)(2,1)S(1)}, u32[]{:S(2)}, u32[]{:S(2)}) collective-permute-start(bf16[256,512]{1,0:T(8,128)(2,1)S(1)} %collective-permute-done.5.a3_ref), channel_id=1, source_target_pairs={{0,8},{4,12},{8,0},{12,4},{16,24},{20,28},{24,16},{28,20},{32,40},... | collective-permute-start | bytes 786440 | tf_op jit(solution)/shard_map/ppermute | solution.py:268
  69.4 4.2 %collective-permute-start.11 = (bf16[256,512]{1,0:T(8,128)(2,1)S(1)}, bf16[256,512]{1,0:T(8,128)(2,1)S(1)}, u32[]{:S(2)}, u32[]{:S(2)}) collective-permute-start(bf16[256,512]{1,0:T(8,128)(2,1)S(1)} %shard_map.98), channel_id=1, source_target_pairs={{0,4},{4,0},{8,12},{12,8},{16,20},{20,16},{24,28},{28,24},{32,36},... | collective-permute-start | bytes 786440 | tf_op jit(solution)/shard_map/ppermute | solution.py:285

commit v4 on v3

--- a/solution.py
+++ b/solution.py
@@ -21,7 +21,6 @@
 COLS = 512
 HEADS = COLS // HD
 VMEM = 48 * 1024 * 1024
-PREP_VMEM = 60 * 1024 * 1024
 NT = (((1,), (1,)), ((), ()))
 TN = (((0,), (0,)), ((), ()))
 bf16, f32 = jnp.bfloat16, jnp.float32
@@ -67,13 +66,10 @@
     return (slot == rank).astype(bf16)
 
 
-def _prepare_kernel(
-    depths_any, grad_any, weight_any, copies_ref, keep_ref, send_ref, q_ref, o_ref, depths_ref, grad_ref, weight_ref, sems
-):
+def _cotangent_kernel(depths_any, grad_any, keep_ref, send_ref, q_ref, o_ref, depths_ref, grad_ref, sems):
     loads = [
         pltpu.make_async_copy(depths_any, depths_ref, sems.at[0]),
-        pltpu.make_async_copy(weight_any, weight_ref, sems.at[1]),
-        pltpu.make_async_copy(grad_any, grad_ref, sems.at[2]),
+        pltpu.make_async_copy(grad_any, grad_ref, sems.at[1]),
     ]
     for load in loads:
         load.start()
@@ -90,9 +86,6 @@
     loads[0].wait()
     sel = _selection(depths_ref[:, pl.ds(pl.multiple_of(x * GROUP, GROUP), GROUP)])
     loads[1].wait()
-    for z in range(NZ):
-        copies_ref[z] = weight_ref[...]
-    loads[2].wait()
     rows = _dot(sel, grad_ref[0]).astype(bf16)
     for n in range(D // 256):
         at = slice(n * 128, (n + 1) * 128)
@@ -223,35 +216,34 @@
         copy.wait()
 
 
-def _call(kernel, outs, flops, nbytes, exps=0, scratch=(), vmem=VMEM, **specs):
+def _call(kernel, outs, flops, nbytes, exps=0, scratch=(), **specs):
     return pl.pallas_call(
         kernel,
         out_shape=tuple(jax.ShapeDtypeStruct(s, t) for s, t in outs),
         scratch_shapes=scratch,
         **specs,
-        compiler_params=pltpu.CompilerParams(vmem_limit_bytes=vmem),
+        compiler_params=pltpu.CompilerParams(vmem_limit_bytes=VMEM),
         cost_estimate=pl.CostEstimate(flops=flops, bytes_accessed=nbytes, transcendentals=exps),
     )
 
 
 def on_device(queries, key_states, value_states, grad_out, out_weight, depths, documents):
-    copies, keep, send = _call(
-        _prepare_kernel,
-        [((NZ, D // (NY * NZ * 2), COLS), bf16)] + [((CAP, KC), bf16)] * 2,
+    keep, send = _call(
+        _cotangent_kernel,
+        [((CAP, KC), bf16)] * 2,
         2 * CAP * D * (GROUP + 256),
         2 << 20,
         scratch=[pltpu.VMEM((CAP, KC), bf16)] * 2
         + [
             pltpu.VMEM((1, SEQ), jnp.int32),
             pltpu.VMEM((1, GROUP, D), bf16),
-            pltpu.VMEM((D // (NY * NZ * 2), COLS), bf16),
-            pltpu.SemaphoreType.DMA((3,)),
+            pltpu.SemaphoreType.DMA((2,)),
         ],
-        vmem=PREP_VMEM,
-        in_specs=[pl.BlockSpec(memory_space=pl.ANY)] * 3,
-    )(depths, grad_out, out_weight)
-    got = lax.ppermute(send, "dp", SWAP)
-    g0 = jnp.concatenate([keep, got], axis=0)
+        in_specs=[pl.BlockSpec(memory_space=pl.ANY)] * 2,
+    )(depths, grad_out)
+    got = [lax.ppermute(send[n * CAP // 2 : (n + 1) * CAP // 2], "dp", SWAP) for n in range(2)]
+    g0 = jnp.concatenate([keep, *got], axis=0)
+    copies = jnp.broadcast_to(out_weight[None], (NZ,) + out_weight.shape)
     own = lax.all_to_all(copies, "dp", 0, 0, axis_index_groups=Z_GROUPS).reshape(HALF, COLS)
     g1 = lax.ppermute(g0, ("dp", "seq"), X_ALONG)
     g3 = lax.ppermute(g0, ("dp", "seq"), X_AGAINST)

time: 76.9 us -> 73.9 us (0.961)
  waiting for transfers between devices: 12.9 us -> 7.96 us
  starting transfers between devices: 52.3 us -> 54.4 us
  Pallas kernels: 8.92 us -> 7.13 us
  local copies, waits for them, and re-layouts: 1.1 us -> 2.79 us
    all_to_all x1, waiting for transfers between devices: 6.86 us -> 0.01 us  [on_device(): lax.all_to_all(copies, 'dp', 0, 0, axis_index_groups=Z_GROUPS)]
    all_to_all x1, starting transfers between devices: 4.81 us -> 11 us  [on_device(): lax.all_to_all(copies, 'dp', 0, 0, axis_index_groups=Z_GROUPS)]
    ppermute x1 -> x2, starting transfers between devices: 8.79 us -> 4.92 us  [on_device(): lax.ppermute(send[n * CAP // 2:(n + 1) * CAP // 2], 'dp', SWAP)]
    ppermute x1, starting transfers between devices: 1.92 us -> 3.88 us  [on_device(): b1 = lax.ppermute(a1, 'dp', Z_SWAP)]
    pallas_call x1, Pallas kernels: 2.79 us -> 1.03 us  [on_device(): _call(_cotangent_kernel, [((CAP, KC), bf16)] * 2, 2 * CAP * D * (GROUP +...]
    ppermute x1, starting transfers between devices: 4.39 us -> 2.79 us  [on_device(): g2 = lax.ppermute(g1, ('dp', 'seq'), X_ALONG)]
    broadcast_in_dim x0 -> x1, local copies, waits for them, and re-layouts: none -> 1.48 us  [on_device(): copies = jnp.broadcast_to(out_weight[None], (NZ,) + out_weight.shape)]
    ppermute x1 -> x2, waiting for transfers between devices: 0.01 us -> 1.27 us  [on_device(): lax.ppermute(send[n * CAP // 2:(n + 1) * CAP // 2], 'dp', SWAP)]
  transfers between devices with their start and end apart: 13 -> 14, of which waited for: 6 -> 5; matrix products, arithmetic and copies ran while one was open for 1% -> 0% of each run, Pallas kernels for 4% -> 6%
where the time goes in v4:
time: 73.9 us; the launch traced here: 73.3 us
  starting transfers between devices  54.4 us (74%)
  waiting for transfers between devices  7.96 us (11%)
  Pallas kernels  7.13 us (10%)
  local copies, waits for them, and re-layouts  2.79 us (4%)
  between operations  0.94 us (1%)
    all_to_all x1, starting transfers between devices, on_device(): lax.all_to_all(copies, 'dp', 0, 0, axis_index_groups=Z_GROUPS)  11 us
    ppermute x1, starting transfers between devices, on_device(): a1 = lax.ppermute(own, 'dp', Y_FIRST)  5.1 us
    ppermute x1, starting transfers between devices, on_device(): a2 = lax.ppermute(a1, 'dp', Y_ALONG)  5.01 us
    ppermute x2, starting transfers between devices, on_device(): lax.ppermute(send[n * CAP // 2:(n + 1) * CAP // 2], 'dp', SWAP)  4.92 us
    ppermute x1, starting transfers between devices, on_device(): g1 = lax.ppermute(g0, ('dp', 'seq'), X_ALONG)  4.39 us
    ppermute x1, starting transfers between devices, on_device(): b1 = lax.ppermute(a1, 'dp', Z_SWAP)  3.88 us
    ppermute x1, starting transfers between devices, on_device(): a4 = lax.ppermute(a3, 'dp', Y_ALONG)  3.64 us
    ppermute x1, starting transfers between devices, on_device(): b2 = lax.ppermute(a2, 'dp', Z_SWAP)  3.37 us
  transfers between devices with their start and end apart: 14, of which 5 were waited for; matrix products, arithmetic and copies ran while one was open for 0% of the time, Pallas kernels for 6%

profile of v4, /device:TPU:1, one launch (start us, length us, event | category | flops | bytes accessed | tf_op | source)
XLA Modules:
  0.0 73.3 jit_solution(14275674032333151374)
XLA Ops:
  0.6 1.5 %broadcast_in_dim.2 = bf16[8,32,512]{2,1,0:T(8,128)(2,1)} broadcast(bf16[32,512]{1,0:T(8,128)(2,1)} %param.11), dimensions={1,2} | broadcast | bytes 294912 | tf_op jit(solution)/shard_map/broadcast_in_dim | solution.py:246
  2.1 0.0 copy-start.4
  2.1 11.0 %all-to-all-start = ((bf16[8,32,512]{2,1,0:T(8,128)(2,1)}), bf16[8,32,512]{2,1,0:T(8,128)(2,1)S(1)}, u32[]{:S(2)}, u32[]{:S(2)}) async-start(bf16[8,32,512]{2,1,0:T(8,128)(2,1)} %broadcast_in_dim.2), calls=%async_computation | async-start | bytes 524288 | tf_op jit(solution)/shard_map/all_to_all | solution.py:247
  13.1 0.0 copy-done.4
  13.1 0.0 copy-start
  13.1 1.2 %copy-done = bf16[1,128,4096]{2,1,0:T(8,128)(2,1)S(1)} copy-done((bf16[1,128,4096]{2,1,0:T(8,128)(2,1)S(1)}, bf16[1,128,4096]{2,1,0:T(8,128)(2,1)}, u32[]{:S(2)}) %copy-start) | copy-done | bytes 1048600
  14.3 1.0 %shard_map.94 = (bf16[64,2048]{1,0:T(8,128)(2,1)S(1)}, bf16[64,2048]{1,0:T(8,128)(2,1)S(1)}) custom-call(s32[1,512]{1,0:T(1,128)S(1)} %copy-done.4, bf16[1,128,4096]{2,1,0:T(8,128)(2,1)S(1)} %copy-done), custom_call_target="tpu_custom_call" | custom-call | flops 201326592 | bytes 2097152 | tf_op jit(solution)/shard_map/pallas_call | solution.py:231
  15.4 0.0 copy-start.3
  15.4 0.0 copy-start.5
  15.4 3.0 %collective-permute-start.2 = (bf16[32,2048]{1,0:T(8,128)(2,1)S(1)}, bf16[32,2048]{1,0:T(8,128)(2,1)S(1)}, u32[]{:S(2)}, u32[]{:S(2)}) collective-permute-start(bf16[32,2048]{1,0:T(8,128)(2,1)S(1)} %get-tuple-element.39), channel_id=1, source_target_pairs={{0,4},{4,0},{8,12},{12,8},{16,20},{20,16},{24,28},{28,24},{32,36},... | collective-permute-start | bytes 393224 | tf_op jit(solution)/shard_map/ppermute | solution.py:244
  18.4 1.9 %collective-permute-start.1 = (bf16[32,2048]{1,0:T(8,128)(2,1)S(1)}, bf16[32,2048]{1,0:T(8,128)(2,1)S(1)}, u32[]{:S(2)}, u32[]{:S(2)}) collective-permute-start(bf16[32,2048]{1,0:T(8,128)(2,1)S(1)} %get-tuple-element.40), channel_id=1, source_target_pairs={{0,4},{4,0},{8,12},{12,8},{16,20},{20,16},{24,28},{28,24},{32,36},... | collective-permute-start | bytes 393224 | tf_op jit(solution)/shard_map/ppermute | solution.py:244
  20.4 0.0 copy-start.1
  20.4 0.0 copy-start.2
  20.4 1.3 %collective-permute-done.1 = bf16[32,2048]{1,0:T(8,128)(2,1)S(1)} collective-permute-done((bf16[32,2048]{1,0:T(8,128)(2,1)S(1)}, bf16[32,2048]{1,0:T(8,128)(2,1)S(1)}, u32[]{:S(2)}, u32[]{:S(2)}) %collective-permute-start.1) | collective-permute-done | bytes 131104 | tf_op jit(solution)/shard_map/ppermute | solution.py:244
  21.7 0.0 collective-permute-done.2
  21.7 4.4 %collective-permute-start.3 = (bf16[128,2048]{1,0:T(8,128)(2,1)S(1)}, bf16[128,2048]{1,0:T(8,128)(2,1)S(1)}, u32[]{:S(2)}, u32[]{:S(2)}) collective-permute-start(bf16[128,2048]{1,0:T(8,128)(2,1)S(1)} %constant_dynamic-update-slice_fusion.g0_ref), channel_id=1, source_target_pairs={{0,1},{1,2},{2,3},{3,0},{4,7},{5,4},{6,5},{7,6},{8,9},{9,10},{10,1... | collective-permute-start | bytes 1572872 | tf_op jit(solution)/shard_map/ppermute | solution.py:248
  26.1 0.0 all-to-all-done
  26.1 5.1 %collective-permute-start = (bf16[256,512]{1,0:T(8,128)(2,1)S(1)}, bf16[256,512]{1,0:T(8,128)(2,1)S(1)}, u32[]{:S(2)}, u32[]{:S(2)}) collective-permute-start(bf16[256,512]{1,0:T(8,128)(2,1)S(1)} %bitcast.1), channel_id=1, source_target_pairs={{0,64},{4,452},{8,460},{12,72},{16,80},{20,468},{24,476},{28,88},{... | collective-permute-start | bytes 786440 | tf_op jit(solution)/shard_map/ppermute | solution.py:251
  31.2 1.9 %collective-permute-start.5 = (bf16[128,2048]{1,0:T(8,128)(2,1)S(1)}, bf16[128,2048]{1,0:T(8,128)(2,1)S(1)}, u32[]{:S(2)}, u32[]{:S(2)}) collective-permute-start(bf16[128,2048]{1,0:T(8,128)(2,1)S(1)} %constant_dynamic-update-slice_fusion.g0_ref), channel_id=1, source_target_pairs={{0,3},{1,0},{2,1},{3,2},{4,5},{5,6},{6,7},{7,4},{8,11},{9,8},{10,9... | collective-permute-start | bytes 1572872 | tf_op jit(solution)/shard_map/ppermute | solution.py:249
  33.2 0.0 collective-permute-done.3.g1_ref
  33.2 1.4 %collective-permute-done.a1_ref = bf16[256,512]{1,0:T(8,128)(2,1)S(1)} collective-permute-done((bf16[256,512]{1,0:T(8,128)(2,1)S(1)}, bf16[256,512]{1,0:T(8,128)(2,1)S(1)}, u32[]{:S(2)}, u32[]{:S(2)}) %collective-permute-start) | collective-permute-done | bytes 262176 | tf_op jit(solution)/shard_map/ppermute | solution.py:251
  34.5 5.0 %collective-permute-start.4 = (bf16[256,512]{1,0:T(8,128)(2,1)S(1)}, bf16[256,512]{1,0:T(8,128)(2,1)S(1)}, u32[]{:S(2)}, u32[]{:S(2)}) collective-permute-start(bf16[256,512]{1,0:T(8,128)(2,1)S(1)} %collective-permute-done.a1_ref), channel_id=1, source_target_pairs={{0,64},{4,452},{8,72},{12,460},{16,80},{20,468},{24,88},{28,476},{... | collective-permute-start | bytes 786440 | tf_op jit(solution)/shard_map/ppermute | solution.py:253
  39.6 2.8 %collective-permute-start.8 = (bf16[128,2048]{1,0:T(8,128)(2,1)S(1)}, bf16[128,2048]{1,0:T(8,128)(2,1)S(1)}, u32[]{:S(2)}, u32[]{:S(2)}) collective-permute-start(bf16[128,2048]{1,0:T(8,128)(2,1)S(1)} %collective-permute-done.3.g1_ref), channel_id=1, source_target_pairs={{0,1},{1,2},{2,3},{3,0},{4,7},{5,4},{6,5},{7,6},{8,9},{9,10},{10,1... | collective-permute-start | bytes 1572872 | tf_op jit(solution)/shard_map/ppermute | solution.py:250
  42.4 3.9 %collective-permute-start.7 = (bf16[256,512]{1,0:T(8,128)(2,1)S(1)}, bf16[256,512]{1,0:T(8,128)(2,1)S(1)}, u32[]{:S(2)}, u32[]{:S(2)}) collective-permute-start(bf16[256,512]{1,0:T(8,128)(2,1)S(1)} %collective-permute-done.a1_ref), channel_id=1, source_target_pairs={{0,8},{4,12},{8,0},{12,4},{16,24},{20,28},{24,16},{28,20},{32,40},... | collective-permute-start | bytes 786440 | tf_op jit(solution)/shard_map/ppermute | solution.py:254
  46.2 0.0 collective-permute-done.5.g3_ref
  46.3 0.0 collective-permute-done.4.a2_ref
  46.3 2.7 %collective-permute-start.6 = (bf16[256,512]{1,0:T(8,128)(2,1)S(1)}, bf16[256,512]{1,0:T(8,128)(2,1)S(1)}, u32[]{:S(2)}, u32[]{:S(2)}) collective-permute-start(bf16[256,512]{1,0:T(8,128)(2,1)S(1)} %collective-permute-done.4.a2_ref), channel_id=1, source_target_pairs={{0,64},{4,452},{8,72},{12,460},{16,80},{20,468},{24,88},{28,476},{... | collective-permute-start | bytes 786440 | tf_op jit(solution)/shard_map/ppermute | solution.py:256
  49.0 3.4 %collective-permute-start.9 = (bf16[256,512]{1,0:T(8,128)(2,1)S(1)}, bf16[256,512]{1,0:T(8,128)(2,1)S(1)}, u32[]{:S(2)}, u32[]{:S(2)}) collective-permute-start(bf16[256,512]{1,0:T(8,128)(2,1)S(1)} %collective-permute-done.4.a2_ref), channel_id=1, source_target_pairs={{0,8},{4,12},{8,0},{12,4},{16,24},{20,28},{24,16},{28,20},{32,40},... | collective-permute-start | bytes 786440 | tf_op jit(solution)/shard_map/ppermute | solution.py:257
  52.4 0.0 collective-permute-done.7.b1_ref
  52.4 0.0 collective-permute-done.8.g2_ref
  52.4 1.3 %collective-permute-done.6.a3_ref = bf16[256,512]{1,0:T(8,128)(2,1)S(1)} collective-permute-done((bf16[256,512]{1,0:T(8,128)(2,1)S(1)}, bf16[256,512]{1,0:T(8,128)(2,1)S(1)}, u32[]{:S(2)}, u32[]{:S(2)}) %collective-permute-start.6) | collective-permute-done | bytes 262176 | tf_op jit(solution)/shard_map/ppermute | solution.py:256
  53.7 3.6 %collective-permute-start.11 = (bf16[256,512]{1,0:T(8,128)(2,1)S(1)}, bf16[256,512]{1,0:T(8,128)(2,1)S(1)}, u32[]{:S(2)}, u32[]{:S(2)}) collective-permute-start(bf16[256,512]{1,0:T(8,128)(2,1)S(1)} %collective-permute-done.6.a3_ref), channel_id=1, source_target_pairs={{0,64},{4,452},{8,72},{12,460},{16,80},{20,468},{24,88},{28,476},{... | collective-permute-start | bytes 786440 | tf_op jit(solution)/shard_map/ppermute | solution.py:259
  57.3 3.4 %collective-permute-start.10 = (bf16[256,512]{1,0:T(8,128)(2,1)S(1)}, bf16[256,512]{1,0:T(8,128)(2,1)S(1)}, u32[]{:S(2)}, u32[]{:S(2)}) collective-permute-start(bf16[256,512]{1,0:T(8,128)(2,1)S(1)} %collective-permute-done.6.a3_ref), channel_id=1, source_target_pairs={{0,8},{4,12},{8,0},{12,4},{16,24},{20,28},{24,16},{28,20},{32,40},... | collective-permute-start | bytes 786440 | tf_op jit(solution)/shard_map/ppermute | solution.py:260
  60.7 0.0 copy-done.3
  60.7 0.0 copy-done.5
  60.7 0.0 copy-done.1
  60.7 0.0 copy-done.2
  60.7 2.0 %shard_map.96 = (bf16[256,512]{1,0:T(8,128)(2,1)S(1)}, bf16[256,512]{1,0:T(8,128)(2,1)S(1)}, bf16[256,512]{1,0:T(8,128)(2,1)S(1)}, f32[4,256,256]{2,1,0:T(8,128)...) custom-call(s32[1,512]{1,0:T(1,128)S(1)} %copy-done.4, ...), custom_call_target="tpu_custom_call" | custom-call | flops 134217728 | bytes 4194304 | tf_op jit(solution)/shard_map/pallas_call | solution.py:261
  62.8 0.0 collective-permute-done.9.b2_ref
  62.8 0.8 %shard_map.95.first_ref = f32[512,512]{1,0:T(8,128)S(1)} custom-call(bf16[256,512]{1,0:T(8,128)(2,1)S(1)} %bitcast.2, bf16[256,512]{1,0:T(8,128)(2,1)S(1)} %collective-permute-done.a1_ref, bf16[256,512]{1,0:T(8,128)(2,1)S(1)} %collective-permute-done.7.b1_ref, bf16[256,512]{1,0:T(8,128)(2,1)S(1)} %collective-permute-done.4.a2_ref, ...), custom_call_target="tpu_custom_call" | custom-call | flops 671088640 | bytes 5242880 | tf_op jit(solution)/shard_map/pallas_call | solution.py:269
  63.6 0.0 collective-permute-done.11.a4_ref
  63.7 3.3 %collective-permute-done.10.b3_ref = bf16[256,512]{1,0:T(8,128)(2,1)S(1)} collective-permute-done((bf16[256,512]{1,0:T(8,128)(2,1)S(1)}, bf16[256,512]{1,0:T(8,128)(2,1)S(1)}, u32[]{:S(2)}, u32[]{:S(2)}) %collective-permute-start.10) | collective-permute-done | bytes 262176 | tf_op jit(solution)/shard_map/ppermute | solution.py:260
  66.9 0.4 shard_map.98
  67.3 2.3 %collective-permute-start.12 = (bf16[256,512]{1,0:T(8,128)(2,1)S(1)}, bf16[256,512]{1,0:T(8,128)(2,1)S(1)}, u32[]{:S(2)}, u32[]{:S(2)}) collective-permute-start(bf16[256,512]{1,0:T(8,128)(2,1)S(1)} %shard_map.98), channel_id=1, source_target_pairs={{0,4},{4,0},{8,12},{12,8},{16,20},{20,16},{24,28},{28,24},{32,36},... | collective-permute-start | bytes 786440 | tf_op jit(solution)/shard_map/ppermute | solution.py:277
  69.6 0.4 shard_map.97.mine_ref
  70.0 0.8 %collective-permute-done.12.other_ref = bf16[256,512]{1,0:T(8,128)(2,1)S(1)} collective-permute-done((bf16[256,512]{1,0:T(8,128)(2,1)S(1)}, bf16[256,512]{1,0:T(8,128)(2,1)S(1)}, u32[]{:S(2)}, u32[]{:S(2)}) %collective-permute-start.12) | collective-permute-done | bytes 262176 | tf_op jit(solution)/shard_map/ppermute | solution.py:277
  70.8 2.5 %shard_map.99 = (bf16[1,512,512]{2,1,0:T(8,128)(2,1)}, bf16[1,512,512]{2,1,0:T(8,128)(2,1)}, bf16[1,512,512]{2,1,0:T(8,128)(2,1)}) custom-call(f32[256,512]{1,0:T(8,128)S(1)} %shard_map.97.mine_ref, bf16[256,512]{1,0:T(8,128)(2,1)S(1)} %collective-permute-done.12.other_ref, bf16[256,512]{1,0:T(8,128)(2,1)S(1)} %get-tuple-element.32.qc_ref, ...), custom_call_target="tpu_custom_call" | custom-call | flops 335544320 | bytes 5242880 | tf_op jit(solution)/shard_map/pallas_call | solution.py:281
  (4 shorter events, 0.1 us)
Async XLA Ops:
  2.1 11.0 %copy-start.4 = (s32[1,512]{1,0:T(1,128)S(1)}, s32[1,512]{1,0:T(1,128)}, u32[]{:S(2)}) copy-start(s32[1,512]{1,0:T(1,128)} %depths_ref.1) | copy-start | bytes 6148
  2.1 24.0 %all-to-all-start = ((bf16[8,32,512]{2,1,0:T(8,128)(2,1)}), bf16[8,32,512]{2,1,0:T(8,128)(2,1)S(1)}, u32[]{:S(2)}, u32[]{:S(2)}) async-start(bf16[8,32,512]{2,1,0:T(8,128)(2,1)} %broadcast_in_dim.2), calls=%async_computation | async-start | bytes 524288 | tf_op jit(solution)/shard_map/all_to_all | solution.py:247
  13.1 1.2 %copy-start = (bf16[1,128,4096]{2,1,0:T(8,128)(2,1)S(1)}, bf16[1,128,4096]{2,1,0:T(8,128)(2,1)}, u32[]{:S(2)}) copy-start(bf16[1,128,4096]{2,1,0:T(8,128)(2,1)} %grad_any.1) | copy-start | bytes 3145732
  15.4 45.3 %copy-start.3 = (bf16[1,512,512]{2,1,0:T(8,128)(2,1)S(1)}, bf16[1,512,512]{2,1,0:T(8,128)(2,1)}, u32[]{:S(2)}) copy-start(bf16[1,512,512]{2,1,0:T(8,128)(2,1)} %v_ref.1) | copy-start | bytes 1572868
  15.4 45.3 %copy-start.5 = (s32[1,512]{1,0:T(1,128)S(1)}, s32[1,512]{1,0:T(1,128)}, u32[]{:S(2)}) copy-start(s32[1,512]{1,0:T(1,128)} %documents_ref.1) | copy-start | bytes 6148
  15.4 6.3 %collective-permute-start.2 = (bf16[32,2048]{1,0:T(8,128)(2,1)S(1)}, bf16[32,2048]{1,0:T(8,128)(2,1)S(1)}, u32[]{:S(2)}, u32[]{:S(2)}) collective-permute-start(bf16[32,2048]{1,0:T(8,128)(2,1)S(1)} %get-tuple-element.39), channel_id=1, source_target_pairs={{0,4},{4,0},{8,12},{12,8},{16,20},{20,16},{24,28},{28,24},{32,36},... | collective-permute-start | bytes 393224 | tf_op jit(solution)/shard_map/ppermute | solution.py:244
  18.4 3.2 %collective-permute-start.1 = (bf16[32,2048]{1,0:T(8,128)(2,1)S(1)}, bf16[32,2048]{1,0:T(8,128)(2,1)S(1)}, u32[]{:S(2)}, u32[]{:S(2)}) collective-permute-start(bf16[32,2048]{1,0:T(8,128)(2,1)S(1)} %get-tuple-element.40), channel_id=1, source_target_pairs={{0,4},{4,0},{8,12},{12,8},{16,20},{20,16},{24,28},{28,24},{32,36},... | collective-permute-start | bytes 393224 | tf_op jit(solution)/shard_map/ppermute | solution.py:244
  20.4 40.4 %copy-start.1 = (bf16[1,512,512]{2,1,0:T(8,128)(2,1)S(1)}, bf16[1,512,512]{2,1,0:T(8,128)(2,1)}, u32[]{:S(2)}) copy-start(bf16[1,512,512]{2,1,0:T(8,128)(2,1)} %q_ref.1) | copy-start | bytes 1572868
  20.4 40.4 %copy-start.2 = (bf16[1,512,512]{2,1,0:T(8,128)(2,1)S(1)}, bf16[1,512,512]{2,1,0:T(8,128)(2,1)}, u32[]{:S(2)}) copy-start(bf16[1,512,512]{2,1,0:T(8,128)(2,1)} %k_ref.1) | copy-start | bytes 1572868
  21.7 11.4 %collective-permute-start.3 = (bf16[128,2048]{1,0:T(8,128)(2,1)S(1)}, bf16[128,2048]{1,0:T(8,128)(2,1)S(1)}, u32[]{:S(2)}, u32[]{:S(2)}) collective-permute-start(bf16[128,2048]{1,0:T(8,128)(2,1)S(1)} %constant_dynamic-update-slice_fusion.g0_ref), channel_id=1, source_target_pairs={{0,1},{1,2},{2,3},{3,0},{4,7},{5,4},{6,5},{7,6},{8,9},{9,10},{10,1... | collective-permute-start | bytes 1572872 | tf_op jit(solution)/shard_map/ppermute | solution.py:248
  26.1 8.4 %collective-permute-start = (bf16[256,512]{1,0:T(8,128)(2,1)S(1)}, bf16[256,512]{1,0:T(8,128)(2,1)S(1)}, u32[]{:S(2)}, u32[]{:S(2)}) collective-permute-start(bf16[256,512]{1,0:T(8,128)(2,1)S(1)} %bitcast.1), channel_id=1, source_target_pairs={{0,64},{4,452},{8,460},{12,72},{16,80},{20,468},{24,476},{28,88},{... | collective-permute-start | bytes 786440 | tf_op jit(solution)/shard_map/ppermute | solution.py:251
  31.2 15.0 %collective-permute-start.5 = (bf16[128,2048]{1,0:T(8,128)(2,1)S(1)}, bf16[128,2048]{1,0:T(8,128)(2,1)S(1)}, u32[]{:S(2)}, u32[]{:S(2)}) collective-permute-start(bf16[128,2048]{1,0:T(8,128)(2,1)S(1)} %constant_dynamic-update-slice_fusion.g0_ref), channel_id=1, source_target_pairs={{0,3},{1,0},{2,1},{3,2},{4,5},{5,6},{6,7},{7,4},{8,11},{9,8},{10,9... | collective-permute-start | bytes 1572872 | tf_op jit(solution)/shard_map/ppermute | solution.py:249
  34.5 11.7 %collective-permute-start.4 = (bf16[256,512]{1,0:T(8,128)(2,1)S(1)}, bf16[256,512]{1,0:T(8,128)(2,1)S(1)}, u32[]{:S(2)}, u32[]{:S(2)}) collective-permute-start(bf16[256,512]{1,0:T(8,128)(2,1)S(1)} %collective-permute-done.a1_ref), channel_id=1, source_target_pairs={{0,64},{4,452},{8,72},{12,460},{16,80},{20,468},{24,88},{28,476},{... | collective-permute-start | bytes 786440 | tf_op jit(solution)/shard_map/ppermute | solution.py:253
  39.6 12.9 %collective-permute-start.8 = (bf16[128,2048]{1,0:T(8,128)(2,1)S(1)}, bf16[128,2048]{1,0:T(8,128)(2,1)S(1)}, u32[]{:S(2)}, u32[]{:S(2)}) collective-permute-start(bf16[128,2048]{1,0:T(8,128)(2,1)S(1)} %collective-permute-done.3.g1_ref), channel_id=1, source_target_pairs={{0,1},{1,2},{2,3},{3,0},{4,7},{5,4},{6,5},{7,6},{8,9},{9,10},{10,1... | collective-permute-start | bytes 1572872 | tf_op jit(solution)/shard_map/ppermute | solution.py:250
  42.4 10.0 %collective-permute-start.7 = (bf16[256,512]{1,0:T(8,128)(2,1)S(1)}, bf16[256,512]{1,0:T(8,128)(2,1)S(1)}, u32[]{:S(2)}, u32[]{:S(2)}) collective-permute-start(bf16[256,512]{1,0:T(8,128)(2,1)S(1)} %collective-permute-done.a1_ref), channel_id=1, source_target_pairs={{0,8},{4,12},{8,0},{12,4},{16,24},{20,28},{24,16},{28,20},{32,40},... | collective-permute-start | bytes 786440 | tf_op jit(solution)/shard_map/ppermute | solution.py:254
  46.3 7.4 %collective-permute-start.6 = (bf16[256,512]{1,0:T(8,128)(2,1)S(1)}, bf16[256,512]{1,0:T(8,128)(2,1)S(1)}, u32[]{:S(2)}, u32[]{:S(2)}) collective-permute-start(bf16[256,512]{1,0:T(8,128)(2,1)S(1)} %collective-permute-done.4.a2_ref), channel_id=1, source_target_pairs={{0,64},{4,452},{8,72},{12,460},{16,80},{20,468},{24,88},{28,476},{... | collective-permute-start | bytes 786440 | tf_op jit(solution)/shard_map/ppermute | solution.py:256
  49.0 13.8 %collective-permute-start.9 = (bf16[256,512]{1,0:T(8,128)(2,1)S(1)}, bf16[256,512]{1,0:T(8,128)(2,1)S(1)}, u32[]{:S(2)}, u32[]{:S(2)}) collective-permute-start(bf16[256,512]{1,0:T(8,128)(2,1)S(1)} %collective-permute-done.4.a2_ref), channel_id=1, source_target_pairs={{0,8},{4,12},{8,0},{12,4},{16,24},{20,28},{24,16},{28,20},{32,40},... | collective-permute-start | bytes 786440 | tf_op jit(solution)/shard_map/ppermute | solution.py:257
  53.7 10.0 %collective-permute-start.11 = (bf16[256,512]{1,0:T(8,128)(2,1)S(1)}, bf16[256,512]{1,0:T(8,128)(2,1)S(1)}, u32[]{:S(2)}, u32[]{:S(2)}) collective-permute-start(bf16[256,512]{1,0:T(8,128)(2,1)S(1)} %collective-permute-done.6.a3_ref), channel_id=1, source_target_pairs={{0,64},{4,452},{8,72},{12,460},{16,80},{20,468},{24,88},{28,476},{... | collective-permute-start | bytes 786440 | tf_op jit(solution)/shard_map/ppermute | solution.py:259
  57.3 9.6 %collective-permute-start.10 = (bf16[256,512]{1,0:T(8,128)(2,1)S(1)}, bf16[256,512]{1,0:T(8,128)(2,1)S(1)}, u32[]{:S(2)}, u32[]{:S(2)}) collective-permute-start(bf16[256,512]{1,0:T(8,128)(2,1)S(1)} %collective-permute-done.6.a3_ref), channel_id=1, source_target_pairs={{0,8},{4,12},{8,0},{12,4},{16,24},{20,28},{24,16},{28,20},{32,40},... | collective-permute-start | bytes 786440 | tf_op jit(solution)/shard_map/ppermute | solution.py:260
  67.3 3.5 %collective-permute-start.12 = (bf16[256,512]{1,0:T(8,128)(2,1)S(1)}, bf16[256,512]{1,0:T(8,128)(2,1)S(1)}, u32[]{:S(2)}, u32[]{:S(2)}) collective-permute-start(bf16[256,512]{1,0:T(8,128)(2,1)S(1)} %shard_map.98), channel_id=1, source_target_pairs={{0,4},{4,0},{8,12},{12,8},{16,20},{20,16},{24,28},{28,24},{32,36},... | collective-permute-start | bytes 786440 | tf_op jit(solution)/shard_map/ppermute | solution.py:277

commit v5 on v4

--- a/solution.py
+++ b/solution.py
@@ -243,7 +243,7 @@
     )(depths, grad_out)
     got = [lax.ppermute(send[n * CAP // 2 : (n + 1) * CAP // 2], "dp", SWAP) for n in range(2)]
     g0 = jnp.concatenate([keep, *got], axis=0)
-    copies = jnp.broadcast_to(out_weight[None], (NZ,) + out_weight.shape)
+    copies = jnp.stack([out_weight] * NZ)
     own = lax.all_to_all(copies, "dp", 0, 0, axis_index_groups=Z_GROUPS).reshape(HALF, COLS)
     g1 = lax.ppermute(g0, ("dp", "seq"), X_ALONG)
     g3 = lax.ppermute(g0, ("dp", "seq"), X_AGAINST)
@@ -255,7 +255,7 @@
     a2, g3 = lax.optimization_barrier((a2, g3))
     a3 = lax.ppermute(a2, "dp", Y_ALONG)
     b2 = lax.ppermute(a2, "dp", Z_SWAP)
-    a3, b1, g2 = lax.optimization_barrier((a3, b1, g2))
+    a3, b1 = lax.optimization_barrier((a3, b1))
     a4 = lax.ppermute(a3, "dp", Y_ALONG)
     b3 = lax.ppermute(a3, "dp", Z_SWAP)
     qc, kc, vc, probs, turned, attended, place = _call(

time: 73.9 us -> 73.9 us (level)
    another operation x0 -> x1, local copies, waits for them, and re-layouts: none -> 1.48 us  [on_device(): copies = jnp.stack([out_weight] * NZ)]
    broadcast_in_dim x1 -> x0, local copies, waits for them, and re-layouts: 1.48 us -> none  [on_device(): copies = jnp.broadcast_to(out_weight[None], (NZ,) + out_weight.shape)]
where the time goes in v5:
time: 73.9 us; the launch traced here: 73.3 us
  starting transfers between devices  54.4 us (74%)
  waiting for transfers between devices  7.96 us (11%)
  Pallas kernels  7.13 us (10%)
  local copies, waits for them, and re-layouts  2.79 us (4%)
  between operations  0.94 us (1%)
    all_to_all x1, starting transfers between devices, on_device(): lax.all_to_all(copies, 'dp', 0, 0, axis_index_groups=Z_GROUPS)  11 us
    ppermute x1, starting transfers between devices, on_device(): a1 = lax.ppermute(own, 'dp', Y_FIRST)  5.1 us
    ppermute x1, starting transfers between devices, on_device(): a2 = lax.ppermute(a1, 'dp', Y_ALONG)  5.01 us
    ppermute x2, starting transfers between devices, on_device(): lax.ppermute(send[n * CAP // 2:(n + 1) * CAP // 2], 'dp', SWAP)  4.92 us
    ppermute x1, starting transfers between devices, on_device(): g1 = lax.ppermute(g0, ('dp', 'seq'), X_ALONG)  4.39 us
    ppermute x1, starting transfers between devices, on_device(): b1 = lax.ppermute(a1, 'dp', Z_SWAP)  3.88 us
    ppermute x1, starting transfers between devices, on_device(): a4 = lax.ppermute(a3, 'dp', Y_ALONG)  3.64 us
    ppermute x1, starting transfers between devices, on_device(): b2 = lax.ppermute(a2, 'dp', Z_SWAP)  3.37 us
  transfers between devices with their start and end apart: 14, of which 5 were waited for; matrix products, arithmetic and copies ran while one was open for 0% of the time, Pallas kernels for 6%

profile of v5, /device:TPU:1, one launch (start us, length us, event | category | flops | bytes accessed | tf_op | source)
XLA Modules:
  0.0 73.3 jit_solution(17389752627140424813)
XLA Ops:
  0.6 1.5 %stack.2 = bf16[8,32,512]{2,1,0:T(8,128)(2,1)} broadcast(bf16[32,512]{1,0:T(8,128)(2,1)} %param.11), dimensions={1,2} | broadcast | bytes 294912 | tf_op jit(solution)/shard_map/stack | solution.py:246
  2.1 0.0 copy-start.4
  2.1 11.0 %all-to-all-start = ((bf16[8,32,512]{2,1,0:T(8,128)(2,1)}), bf16[8,32,512]{2,1,0:T(8,128)(2,1)S(1)}, u32[]{:S(2)}, u32[]{:S(2)}) async-start(bf16[8,32,512]{2,1,0:T(8,128)(2,1)} %stack.2), calls=%async_computation | async-start | bytes 524288 | tf_op jit(solution)/shard_map/all_to_all | solution.py:247
  13.1 0.0 copy-done.4
  13.1 0.0 copy-start
  13.1 1.2 %copy-done = bf16[1,128,4096]{2,1,0:T(8,128)(2,1)S(1)} copy-done((bf16[1,128,4096]{2,1,0:T(8,128)(2,1)S(1)}, bf16[1,128,4096]{2,1,0:T(8,128)(2,1)}, u32[]{:S(2)}) %copy-start) | copy-done | bytes 1048600
  14.3 1.0 %shard_map.94 = (bf16[64,2048]{1,0:T(8,128)(2,1)S(1)}, bf16[64,2048]{1,0:T(8,128)(2,1)S(1)}) custom-call(s32[1,512]{1,0:T(1,128)S(1)} %copy-done.4, bf16[1,128,4096]{2,1,0:T(8,128)(2,1)S(1)} %copy-done), custom_call_target="tpu_custom_call" | custom-call | flops 201326592 | bytes 2097152 | tf_op jit(solution)/shard_map/pallas_call | solution.py:231
  15.4 0.0 copy-start.3
  15.4 0.0 copy-start.5
  15.4 3.0 %collective-permute-start.2 = (bf16[32,2048]{1,0:T(8,128)(2,1)S(1)}, bf16[32,2048]{1,0:T(8,128)(2,1)S(1)}, u32[]{:S(2)}, u32[]{:S(2)}) collective-permute-start(bf16[32,2048]{1,0:T(8,128)(2,1)S(1)} %get-tuple-element.37), channel_id=1, source_target_pairs={{0,4},{4,0},{8,12},{12,8},{16,20},{20,16},{24,28},{28,24},{32,36},... | collective-permute-start | bytes 393224 | tf_op jit(solution)/shard_map/ppermute | solution.py:244
  18.4 1.9 %collective-permute-start.1 = (bf16[32,2048]{1,0:T(8,128)(2,1)S(1)}, bf16[32,2048]{1,0:T(8,128)(2,1)S(1)}, u32[]{:S(2)}, u32[]{:S(2)}) collective-permute-start(bf16[32,2048]{1,0:T(8,128)(2,1)S(1)} %get-tuple-element.38), channel_id=1, source_target_pairs={{0,4},{4,0},{8,12},{12,8},{16,20},{20,16},{24,28},{28,24},{32,36},... | collective-permute-start | bytes 393224 | tf_op jit(solution)/shard_map/ppermute | solution.py:244
  20.4 0.0 copy-start.1
  20.4 0.0 copy-start.2
  20.4 1.3 %collective-permute-done.1 = bf16[32,2048]{1,0:T(8,128)(2,1)S(1)} collective-permute-done((bf16[32,2048]{1,0:T(8,128)(2,1)S(1)}, bf16[32,2048]{1,0:T(8,128)(2,1)S(1)}, u32[]{:S(2)}, u32[]{:S(2)}) %collective-permute-start.1) | collective-permute-done | bytes 131104 | tf_op jit(solution)/shard_map/ppermute | solution.py:244
  21.7 0.0 collective-permute-done.2
  21.7 4.4 %collective-permute-start.3 = (bf16[128,2048]{1,0:T(8,128)(2,1)S(1)}, bf16[128,2048]{1,0:T(8,128)(2,1)S(1)}, u32[]{:S(2)}, u32[]{:S(2)}) collective-permute-start(bf16[128,2048]{1,0:T(8,128)(2,1)S(1)} %constant_dynamic-update-slice_fusion.g0_ref), channel_id=1, source_target_pairs={{0,1},{1,2},{2,3},{3,0},{4,7},{5,4},{6,5},{7,6},{8,9},{9,10},{10,1... | collective-permute-start | bytes 1572872 | tf_op jit(solution)/shard_map/ppermute | solution.py:248
  26.1 0.0 all-to-all-done
  26.1 5.1 %collective-permute-start = (bf16[256,512]{1,0:T(8,128)(2,1)S(1)}, bf16[256,512]{1,0:T(8,128)(2,1)S(1)}, u32[]{:S(2)}, u32[]{:S(2)}) collective-permute-start(bf16[256,512]{1,0:T(8,128)(2,1)S(1)} %bitcast.1), channel_id=1, source_target_pairs={{0,64},{4,452},{8,460},{12,72},{16,80},{20,468},{24,476},{28,88},{... | collective-permute-start | bytes 786440 | tf_op jit(solution)/shard_map/ppermute | solution.py:251
  31.2 1.9 %collective-permute-start.5 = (bf16[128,2048]{1,0:T(8,128)(2,1)S(1)}, bf16[128,2048]{1,0:T(8,128)(2,1)S(1)}, u32[]{:S(2)}, u32[]{:S(2)}) collective-permute-start(bf16[128,2048]{1,0:T(8,128)(2,1)S(1)} %constant_dynamic-update-slice_fusion.g0_ref), channel_id=1, source_target_pairs={{0,3},{1,0},{2,1},{3,2},{4,5},{5,6},{6,7},{7,4},{8,11},{9,8},{10,9... | collective-permute-start | bytes 1572872 | tf_op jit(solution)/shard_map/ppermute | solution.py:249
  33.2 0.0 collective-permute-done.3.g1_ref
  33.2 1.4 %collective-permute-done.a1_ref = bf16[256,512]{1,0:T(8,128)(2,1)S(1)} collective-permute-done((bf16[256,512]{1,0:T(8,128)(2,1)S(1)}, bf16[256,512]{1,0:T(8,128)(2,1)S(1)}, u32[]{:S(2)}, u32[]{:S(2)}) %collective-permute-start) | collective-permute-done | bytes 262176 | tf_op jit(solution)/shard_map/ppermute | solution.py:251
  34.5 5.0 %collective-permute-start.4 = (bf16[256,512]{1,0:T(8,128)(2,1)S(1)}, bf16[256,512]{1,0:T(8,128)(2,1)S(1)}, u32[]{:S(2)}, u32[]{:S(2)}) collective-permute-start(bf16[256,512]{1,0:T(8,128)(2,1)S(1)} %collective-permute-done.a1_ref), channel_id=1, source_target_pairs={{0,64},{4,452},{8,72},{12,460},{16,80},{20,468},{24,88},{28,476},{... | collective-permute-start | bytes 786440 | tf_op jit(solution)/shard_map/ppermute | solution.py:253
  39.6 2.8 %collective-permute-start.9 = (bf16[128,2048]{1,0:T(8,128)(2,1)S(1)}, bf16[128,2048]{1,0:T(8,128)(2,1)S(1)}, u32[]{:S(2)}, u32[]{:S(2)}) collective-permute-start(bf16[128,2048]{1,0:T(8,128)(2,1)S(1)} %collective-permute-done.3.g1_ref), channel_id=1, source_target_pairs={{0,1},{1,2},{2,3},{3,0},{4,7},{5,4},{6,5},{7,6},{8,9},{9,10},{10,1... | collective-permute-start | bytes 1572872 | tf_op jit(solution)/shard_map/ppermute | solution.py:250
  42.4 3.9 %collective-permute-start.7 = (bf16[256,512]{1,0:T(8,128)(2,1)S(1)}, bf16[256,512]{1,0:T(8,128)(2,1)S(1)}, u32[]{:S(2)}, u32[]{:S(2)}) collective-permute-start(bf16[256,512]{1,0:T(8,128)(2,1)S(1)} %collective-permute-done.a1_ref), channel_id=1, source_target_pairs={{0,8},{4,12},{8,0},{12,4},{16,24},{20,28},{24,16},{28,20},{32,40},... | collective-permute-start | bytes 786440 | tf_op jit(solution)/shard_map/ppermute | solution.py:254
  46.2 0.0 collective-permute-done.5.g3_ref
  46.3 0.0 collective-permute-done.4.a2_ref
  46.3 2.7 %collective-permute-start.6 = (bf16[256,512]{1,0:T(8,128)(2,1)S(1)}, bf16[256,512]{1,0:T(8,128)(2,1)S(1)}, u32[]{:S(2)}, u32[]{:S(2)}) collective-permute-start(bf16[256,512]{1,0:T(8,128)(2,1)S(1)} %collective-permute-done.4.a2_ref), channel_id=1, source_target_pairs={{0,64},{4,452},{8,72},{12,460},{16,80},{20,468},{24,88},{28,476},{... | collective-permute-start | bytes 786440 | tf_op jit(solution)/shard_map/ppermute | solution.py:256
  49.0 3.4 %collective-permute-start.8 = (bf16[256,512]{1,0:T(8,128)(2,1)S(1)}, bf16[256,512]{1,0:T(8,128)(2,1)S(1)}, u32[]{:S(2)}, u32[]{:S(2)}) collective-permute-start(bf16[256,512]{1,0:T(8,128)(2,1)S(1)} %collective-permute-done.4.a2_ref), channel_id=1, source_target_pairs={{0,8},{4,12},{8,0},{12,4},{16,24},{20,28},{24,16},{28,20},{32,40},... | collective-permute-start | bytes 786440 | tf_op jit(solution)/shard_map/ppermute | solution.py:257
  52.4 0.0 collective-permute-done.7.b1_ref
  52.4 1.3 %collective-permute-done.6.a3_ref = bf16[256,512]{1,0:T(8,128)(2,1)S(1)} collective-permute-done((bf16[256,512]{1,0:T(8,128)(2,1)S(1)}, bf16[256,512]{1,0:T(8,128)(2,1)S(1)}, u32[]{:S(2)}, u32[]{:S(2)}) %collective-permute-start.6) | collective-permute-done | bytes 262176 | tf_op jit(solution)/shard_map/ppermute | solution.py:256
  53.7 3.6 %collective-permute-start.11 = (bf16[256,512]{1,0:T(8,128)(2,1)S(1)}, bf16[256,512]{1,0:T(8,128)(2,1)S(1)}, u32[]{:S(2)}, u32[]{:S(2)}) collective-permute-start(bf16[256,512]{1,0:T(8,128)(2,1)S(1)} %collective-permute-done.6.a3_ref), channel_id=1, source_target_pairs={{0,64},{4,452},{8,72},{12,460},{16,80},{20,468},{24,88},{28,476},{... | collective-permute-start | bytes 786440 | tf_op jit(solution)/shard_map/ppermute | solution.py:259
  57.3 3.4 %collective-permute-start.10 = (bf16[256,512]{1,0:T(8,128)(2,1)S(1)}, bf16[256,512]{1,0:T(8,128)(2,1)S(1)}, u32[]{:S(2)}, u32[]{:S(2)}) collective-permute-start(bf16[256,512]{1,0:T(8,128)(2,1)S(1)} %collective-permute-done.6.a3_ref), channel_id=1, source_target_pairs={{0,8},{4,12},{8,0},{12,4},{16,24},{20,28},{24,16},{28,20},{32,40},... | collective-permute-start | bytes 786440 | tf_op jit(solution)/shard_map/ppermute | solution.py:260
  60.7 0.0 copy-done.3
  60.7 0.0 copy-done.5
  60.7 0.0 copy-done.1
  60.7 0.0 copy-done.2
  60.7 2.0 %shard_map.96 = (bf16[256,512]{1,0:T(8,128)(2,1)S(1)}, bf16[256,512]{1,0:T(8,128)(2,1)S(1)}, bf16[256,512]{1,0:T(8,128)(2,1)S(1)}, f32[4,256,256]{2,1,0:T(8,128)...) custom-call(s32[1,512]{1,0:T(1,128)S(1)} %copy-done.4, ...), custom_call_target="tpu_custom_call" | custom-call | flops 134217728 | bytes 4194304 | tf_op jit(solution)/shard_map/pallas_call | solution.py:261
  62.8 0.0 collective-permute-done.9.g2_ref
  62.8 0.0 collective-permute-done.8.b2_ref
  62.8 0.8 %shard_map.95.first_ref = f32[512,512]{1,0:T(8,128)S(1)} custom-call(bf16[256,512]{1,0:T(8,128)(2,1)S(1)} %bitcast.2, bf16[256,512]{1,0:T(8,128)(2,1)S(1)} %collective-permute-done.a1_ref, bf16[256,512]{1,0:T(8,128)(2,1)S(1)} %collective-permute-done.7.b1_ref, bf16[256,512]{1,0:T(8,128)(2,1)S(1)} %collective-permute-done.4.a2_ref, ...), custom_call_target="tpu_custom_call" | custom-call | flops 671088640 | bytes 5242880 | tf_op jit(solution)/shard_map/pallas_call | solution.py:269
  63.6 0.0 collective-permute-done.11.a4_ref
  63.7 3.3 %collective-permute-done.10.b3_ref = bf16[256,512]{1,0:T(8,128)(2,1)S(1)} collective-permute-done((bf16[256,512]{1,0:T(8,128)(2,1)S(1)}, bf16[256,512]{1,0:T(8,128)(2,1)S(1)}, u32[]{:S(2)}, u32[]{:S(2)}) %collective-permute-start.10) | collective-permute-done | bytes 262176 | tf_op jit(solution)/shard_map/ppermute | solution.py:260
  66.9 0.4 shard_map.98
  67.3 2.3 %collective-permute-start.12 = (bf16[256,512]{1,0:T(8,128)(2,1)S(1)}, bf16[256,512]{1,0:T(8,128)(2,1)S(1)}, u32[]{:S(2)}, u32[]{:S(2)}) collective-permute-start(bf16[256,512]{1,0:T(8,128)(2,1)S(1)} %shard_map.98), channel_id=1, source_target_pairs={{0,4},{4,0},{8,12},{12,8},{16,20},{20,16},{24,28},{28,24},{32,36},... | collective-permute-start | bytes 786440 | tf_op jit(solution)/shard_map/ppermute | solution.py:277
  69.6 0.4 shard_map.97.mine_ref
  70.0 0.8 %collective-permute-done.12.other_ref = bf16[256,512]{1,0:T(8,128)(2,1)S(1)} collective-permute-done((bf16[256,512]{1,0:T(8,128)(2,1)S(1)}, bf16[256,512]{1,0:T(8,128)(2,1)S(1)}, u32[]{:S(2)}, u32[]{:S(2)}) %collective-permute-start.12) | collective-permute-done | bytes 262176 | tf_op jit(solution)/shard_map/ppermute | solution.py:277
  70.8 2.5 %shard_map.99 = (bf16[1,512,512]{2,1,0:T(8,128)(2,1)}, bf16[1,512,512]{2,1,0:T(8,128)(2,1)}, bf16[1,512,512]{2,1,0:T(8,128)(2,1)}) custom-call(f32[256,512]{1,0:T(8,128)S(1)} %shard_map.97.mine_ref, bf16[256,512]{1,0:T(8,128)(2,1)S(1)} %collective-permute-done.12.other_ref, bf16[256,512]{1,0:T(8,128)(2,1)S(1)} %get-tuple-element.30.qc_ref, ...), custom_call_target="tpu_custom_call" | custom-call | flops 335544320 | bytes 5242880 | tf_op jit(solution)/shard_map/pallas_call | solution.py:281
  (4 shorter events, 0.1 us)
Async XLA Ops:
  2.1 11.0 %copy-start.4 = (s32[1,512]{1,0:T(1,128)S(1)}, s32[1,512]{1,0:T(1,128)}, u32[]{:S(2)}) copy-start(s32[1,512]{1,0:T(1,128)} %depths_ref.1) | copy-start | bytes 6148
  2.1 24.0 %all-to-all-start = ((bf16[8,32,512]{2,1,0:T(8,128)(2,1)}), bf16[8,32,512]{2,1,0:T(8,128)(2,1)S(1)}, u32[]{:S(2)}, u32[]{:S(2)}) async-start(bf16[8,32,512]{2,1,0:T(8,128)(2,1)} %stack.2), calls=%async_computation | async-start | bytes 524288 | tf_op jit(solution)/shard_map/all_to_all | solution.py:247
  13.1 1.2 %copy-start = (bf16[1,128,4096]{2,1,0:T(8,128)(2,1)S(1)}, bf16[1,128,4096]{2,1,0:T(8,128)(2,1)}, u32[]{:S(2)}) copy-start(bf16[1,128,4096]{2,1,0:T(8,128)(2,1)} %grad_any.1) | copy-start | bytes 3145732
  15.4 45.3 %copy-start.3 = (bf16[1,512,512]{2,1,0:T(8,128)(2,1)S(1)}, bf16[1,512,512]{2,1,0:T(8,128)(2,1)}, u32[]{:S(2)}) copy-start(bf16[1,512,512]{2,1,0:T(8,128)(2,1)} %v_ref.1) | copy-start | bytes 1572868
  15.4 45.3 %copy-start.5 = (s32[1,512]{1,0:T(1,128)S(1)}, s32[1,512]{1,0:T(1,128)}, u32[]{:S(2)}) copy-start(s32[1,512]{1,0:T(1,128)} %documents_ref.1) | copy-start | bytes 6148
  15.4 6.3 %collective-permute-start.2 = (bf16[32,2048]{1,0:T(8,128)(2,1)S(1)}, bf16[32,2048]{1,0:T(8,128)(2,1)S(1)}, u32[]{:S(2)}, u32[]{:S(2)}) collective-permute-start(bf16[32,2048]{1,0:T(8,128)(2,1)S(1)} %get-tuple-element.37), channel_id=1, source_target_pairs={{0,4},{4,0},{8,12},{12,8},{16,20},{20,16},{24,28},{28,24},{32,36},... | collective-permute-start | bytes 393224 | tf_op jit(solution)/shard_map/ppermute | solution.py:244
  18.4 3.2 %collective-permute-start.1 = (bf16[32,2048]{1,0:T(8,128)(2,1)S(1)}, bf16[32,2048]{1,0:T(8,128)(2,1)S(1)}, u32[]{:S(2)}, u32[]{:S(2)}) collective-permute-start(bf16[32,2048]{1,0:T(8,128)(2,1)S(1)} %get-tuple-element.38), channel_id=1, source_target_pairs={{0,4},{4,0},{8,12},{12,8},{16,20},{20,16},{24,28},{28,24},{32,36},... | collective-permute-start | bytes 393224 | tf_op jit(solution)/shard_map/ppermute | solution.py:244
  20.4 40.4 %copy-start.1 = (bf16[1,512,512]{2,1,0:T(8,128)(2,1)S(1)}, bf16[1,512,512]{2,1,0:T(8,128)(2,1)}, u32[]{:S(2)}) copy-start(bf16[1,512,512]{2,1,0:T(8,128)(2,1)} %q_ref.1) | copy-start | bytes 1572868
  20.4 40.4 %copy-start.2 = (bf16[1,512,512]{2,1,0:T(8,128)(2,1)S(1)}, bf16[1,512,512]{2,1,0:T(8,128)(2,1)}, u32[]{:S(2)}) copy-start(bf16[1,512,512]{2,1,0:T(8,128)(2,1)} %k_ref.1) | copy-start | bytes 1572868
  21.7 11.4 %collective-permute-start.3 = (bf16[128,2048]{1,0:T(8,128)(2,1)S(1)}, bf16[128,2048]{1,0:T(8,128)(2,1)S(1)}, u32[]{:S(2)}, u32[]{:S(2)}) collective-permute-start(bf16[128,2048]{1,0:T(8,128)(2,1)S(1)} %constant_dynamic-update-slice_fusion.g0_ref), channel_id=1, source_target_pairs={{0,1},{1,2},{2,3},{3,0},{4,7},{5,4},{6,5},{7,6},{8,9},{9,10},{10,1... | collective-permute-start | bytes 1572872 | tf_op jit(solution)/shard_map/ppermute | solution.py:248
  26.1 8.4 %collective-permute-start = (bf16[256,512]{1,0:T(8,128)(2,1)S(1)}, bf16[256,512]{1,0:T(8,128)(2,1)S(1)}, u32[]{:S(2)}, u32[]{:S(2)}) collective-permute-start(bf16[256,512]{1,0:T(8,128)(2,1)S(1)} %bitcast.1), channel_id=1, source_target_pairs={{0,64},{4,452},{8,460},{12,72},{16,80},{20,468},{24,476},{28,88},{... | collective-permute-start | bytes 786440 | tf_op jit(solution)/shard_map/ppermute | solution.py:251
  31.2 15.0 %collective-permute-start.5 = (bf16[128,2048]{1,0:T(8,128)(2,1)S(1)}, bf16[128,2048]{1,0:T(8,128)(2,1)S(1)}, u32[]{:S(2)}, u32[]{:S(2)}) collective-permute-start(bf16[128,2048]{1,0:T(8,128)(2,1)S(1)} %constant_dynamic-update-slice_fusion.g0_ref), channel_id=1, source_target_pairs={{0,3},{1,0},{2,1},{3,2},{4,5},{5,6},{6,7},{7,4},{8,11},{9,8},{10,9... | collective-permute-start | bytes 1572872 | tf_op jit(solution)/shard_map/ppermute | solution.py:249
  34.5 11.7 %collective-permute-start.4 = (bf16[256,512]{1,0:T(8,128)(2,1)S(1)}, bf16[256,512]{1,0:T(8,128)(2,1)S(1)}, u32[]{:S(2)}, u32[]{:S(2)}) collective-permute-start(bf16[256,512]{1,0:T(8,128)(2,1)S(1)} %collective-permute-done.a1_ref), channel_id=1, source_target_pairs={{0,64},{4,452},{8,72},{12,460},{16,80},{20,468},{24,88},{28,476},{... | collective-permute-start | bytes 786440 | tf_op jit(solution)/shard_map/ppermute | solution.py:253
  39.6 23.2 %collective-permute-start.9 = (bf16[128,2048]{1,0:T(8,128)(2,1)S(1)}, bf16[128,2048]{1,0:T(8,128)(2,1)S(1)}, u32[]{:S(2)}, u32[]{:S(2)}) collective-permute-start(bf16[128,2048]{1,0:T(8,128)(2,1)S(1)} %collective-permute-done.3.g1_ref), channel_id=1, source_target_pairs={{0,1},{1,2},{2,3},{3,0},{4,7},{5,4},{6,5},{7,6},{8,9},{9,10},{10,1... | collective-permute-start | bytes 1572872 | tf_op jit(solution)/shard_map/ppermute | solution.py:250
  42.4 10.0 %collective-permute-start.7 = (bf16[256,512]{1,0:T(8,128)(2,1)S(1)}, bf16[256,512]{1,0:T(8,128)(2,1)S(1)}, u32[]{:S(2)}, u32[]{:S(2)}) collective-permute-start(bf16[256,512]{1,0:T(8,128)(2,1)S(1)} %collective-permute-done.a1_ref), channel_id=1, source_target_pairs={{0,8},{4,12},{8,0},{12,4},{16,24},{20,28},{24,16},{28,20},{32,40},... | collective-permute-start | bytes 786440 | tf_op jit(solution)/shard_map/ppermute | solution.py:254
  46.3 7.4 %collective-permute-start.6 = (bf16[256,512]{1,0:T(8,128)(2,1)S(1)}, bf16[256,512]{1,0:T(8,128)(2,1)S(1)}, u32[]{:S(2)}, u32[]{:S(2)}) collective-permute-start(bf16[256,512]{1,0:T(8,128)(2,1)S(1)} %collective-permute-done.4.a2_ref), channel_id=1, source_target_pairs={{0,64},{4,452},{8,72},{12,460},{16,80},{20,468},{24,88},{28,476},{... | collective-permute-start | bytes 786440 | tf_op jit(solution)/shard_map/ppermute | solution.py:256
  49.0 13.8 %collective-permute-start.8 = (bf16[256,512]{1,0:T(8,128)(2,1)S(1)}, bf16[256,512]{1,0:T(8,128)(2,1)S(1)}, u32[]{:S(2)}, u32[]{:S(2)}) collective-permute-start(bf16[256,512]{1,0:T(8,128)(2,1)S(1)} %collective-permute-done.4.a2_ref), channel_id=1, source_target_pairs={{0,8},{4,12},{8,0},{12,4},{16,24},{20,28},{24,16},{28,20},{32,40},... | collective-permute-start | bytes 786440 | tf_op jit(solution)/shard_map/ppermute | solution.py:257
  53.7 10.0 %collective-permute-start.11 = (bf16[256,512]{1,0:T(8,128)(2,1)S(1)}, bf16[256,512]{1,0:T(8,128)(2,1)S(1)}, u32[]{:S(2)}, u32[]{:S(2)}) collective-permute-start(bf16[256,512]{1,0:T(8,128)(2,1)S(1)} %collective-permute-done.6.a3_ref), channel_id=1, source_target_pairs={{0,64},{4,452},{8,72},{12,460},{16,80},{20,468},{24,88},{28,476},{... | collective-permute-start | bytes 786440 | tf_op jit(solution)/shard_map/ppermute | solution.py:259
  57.3 9.6 %collective-permute-start.10 = (bf16[256,512]{1,0:T(8,128)(2,1)S(1)}, bf16[256,512]{1,0:T(8,128)(2,1)S(1)}, u32[]{:S(2)}, u32[]{:S(2)}) collective-permute-start(bf16[256,512]{1,0:T(8,128)(2,1)S(1)} %collective-permute-done.6.a3_ref), channel_id=1, source_target_pairs={{0,8},{4,12},{8,0},{12,4},{16,24},{20,28},{24,16},{28,20},{32,40},... | collective-permute-start | bytes 786440 | tf_op jit(solution)/shard_map/ppermute | solution.py:260
  67.3 3.5 %collective-permute-start.12 = (bf16[256,512]{1,0:T(8,128)(2,1)S(1)}, bf16[256,512]{1,0:T(8,128)(2,1)S(1)}, u32[]{:S(2)}, u32[]{:S(2)}) collective-permute-start(bf16[256,512]{1,0:T(8,128)(2,1)S(1)} %shard_map.98), channel_id=1, source_target_pairs={{0,4},{4,0},{8,12},{12,8},{16,20},{20,16},{24,28},{28,24},{32,36},... | collective-permute-start | bytes 786440 | tf_op jit(solution)/shard_map/ppermute | solution.py:277
